TPU v7x, 256 devices: a whole 4x4x8 slice. The times are simulated.
256 devices in a mesh: gx: 4 (over y), gy: 8 (over x, core), gz: 8 (over z).
Axes of the slice: x: 4, y: 4, z: 8, core: 2. Of those that a mesh axis runs over, the one named last changes fastest.
Arguments:
- right_side: float32 [64, 256, 1024], P('gx', 'gy', 'gz'), may hold values from -48 to 48
- dielectric: float32 [64, 256, 1024], P('gx', 'gy', 'gz'), may hold values from 1 to 16
- guess: float32 [64, 256, 1024], P('gx', 'gy', 'gz'), may hold values from -1.5 to 1.5
Outputs:
- solution: float32 [64, 256, 1024], P('gx', 'gy', 'gz')
- residual: float32 [64, 256, 1024], P('gx', 'gy', 'gz')
All inputs are finite; a program needn't handle non-finite values.
Results may differ from a plain program's by a relative error of at most 0.0001.
Values sent between devices are 32-bit elements; how exact they have to be, the bound alone decides.
A program may use at most 256 MiB of HBM per device.

v0:
```python
import jax
import jax.numpy as jnp
from jax import lax
from jax.sharding import PartitionSpec as P

LEVELS = 5
COARSE_SWEEPS = 4


OMEGA = 0.8


def extended(cells, sides, width):
    for axis, dim in sides:
        count = lax.axis_size(axis)
        ends = count - 1
        head = lax.slice_in_dim(cells, 0, width, axis=dim)
        tail = lax.slice_in_dim(cells, cells.shape[dim] - width, cells.shape[dim], axis=dim)
        cells = jnp.concatenate(
            [
                lax.ppermute(tail, axis, [(i, (i + 1) % count) for i in range(ends)]),
                cells,
                lax.ppermute(head, axis, [((i + 1) % count, i) for i in range(ends)]),
            ],
            axis=dim,
        )
    return cells


def coarsen(values):
    span_first, span_second, span_third = values.shape
    blocks = values.reshape(span_first // 2, 2, span_second // 2, 2, span_third // 2, 2)
    return jnp.mean(blocks, axis=(1, 3, 5))


def refine(values):
    return jnp.repeat(jnp.repeat(jnp.repeat(values, 2, axis=0), 2, axis=1), 2, axis=2)


def field_rims(values):
    return extended(values, (("gx", 0), ("gy", 1), ("gz", 2)), 1)


def dielectric_rims(values):
    return extended(values, (("gx", 0), ("gy", 1), ("gz", 2)), 1)


def neighbours(padded):
    return [
        padded[:-2, 1:-1, 1:-1],
        padded[2:, 1:-1, 1:-1],
        padded[1:-1, :-2, 1:-1],
        padded[1:-1, 2:, 1:-1],
        padded[1:-1, 1:-1, :-2],
        padded[1:-1, 1:-1, 2:],
    ]


def operator_from(permit_padded, scale):
    center = permit_padded[1:-1, 1:-1, 1:-1]
    couplings = [0.5 * (center + side) for side in neighbours(permit_padded)]
    total = couplings[0]
    for extra in couplings[1:]:
        total = total + extra
    return (couplings, scale * total, scale)


def apply_operator(padded, stencil):
    couplings, diagonal_part, scale = stencil
    center = padded[1:-1, 1:-1, 1:-1]
    sides = neighbours(padded)
    total = couplings[0] * (center - sides[0])
    for index in range(1, 6):
        total = total + couplings[index] * (center - sides[index])
    return scale * total


def relax(values, source, stencil, padder):
    return values + OMEGA * (source - apply_operator(padder(values), stencil)) / stencil[1]


def coarsest(source, stencil, padder):
    values = OMEGA * source / stencil[1]
    for sweep_index in range(COARSE_SWEEPS - 1):
        values = relax(values, source, stencil, padder)
    return values


def cycle(level, source, stencils, padder, bottom):
    if level == len(stencils):
        return bottom(source)
    stencil = stencils[level]
    values = OMEGA * source / stencil[1]
    remainder = source - apply_operator(padder(values), stencil)
    values = values + refine(cycle(level + 1, coarsen(remainder), stencils, padder, bottom))
    return relax(values, source, stencil, padder)


def shards(right_side, dielectric, guess):
    levels = [dielectric]
    for level in range(1, LEVELS):
        levels.append(coarsen(levels[-1]))
    padded_levels = [None] * LEVELS
    padded_levels[0] = dielectric_rims(dielectric)
    guess_padded = field_rims(guess)

    def permit_padded(level):
        if padded_levels[level] is None:
            padded_levels[level] = dielectric_rims(levels[level])
        return padded_levels[level]

    finest = operator_from(permit_padded(0), 1.0)
    smoothed = guess + OMEGA * (right_side - apply_operator(guess_padded, finest)) / finest[1]
    remainder = right_side - apply_operator(field_rims(smoothed), finest)
    stencils = [finest] + [
        operator_from(permit_padded(level), 0.25**level) for level in range(1, LEVELS - 1)
    ]
    lowest = operator_from(permit_padded(LEVELS - 1), 0.25 ** (LEVELS - 1))

    def bottom(source_low):
        return coarsest(source_low, lowest, field_rims)

    correction = cycle(1, coarsen(remainder), stencils, field_rims, bottom)
    solution = relax(smoothed + refine(correction), right_side, finest, field_rims)
    residual = right_side - apply_operator(field_rims(solution), finest)
    return (solution, residual)


def solution(mesh):
    return jax.shard_map(
        shards,
        mesh=mesh,
        in_specs=(P("gx", "gy", "gz"), P("gx", "gy", "gz"), P("gx", "gy", "gz")),
        out_specs=(P("gx", "gy", "gz"), P("gx", "gy", "gz")),
        check_vma=False,
    )
```

profile of v0, /device:TPU:1, one launch (start us, length us, event | category | flops | bytes accessed | tf_op | source)
XLA Modules:
  0.0 502.8 jit_solution(12677080715538650152)
XLA Ops:
  0.6 18.9 %reshape.95 = f32[8,2,16,2,64,2]{5,4,3,2,1,0:T(8,128)} reshape(f32[16,32,128]{2,1,0:T(8,128)} %param.4) | data formatting | bytes 524288 | tf_op jit(solution)/shard_map/reshape | solution.py:32
  19.6 7.0 %reduce_sum.87 = f32[8,16,64]{2,1,0:T(8,128)S(1)} reduce(f32[8,2,16,2,64,2]{5,4,3,2,1,0:T(8,128)} %reshape.95, f32[]{:T(128)} %constant.14.clone.1), dimensions={1,3,5}, to_apply=%region_1.0 | reduce | flops 57344 | bytes 294916 | tf_op jit(solution)/shard_map/reduce_sum | solution.py:33
  30.8 4.7 collective-permute-start.54
  42.3 5.6 %collective-permute-start.57 = (f32[3,1,8]{2,1,0:T(1,128)S(1)}, f32[3,1,8]{2,1,0:T(1,128)S(1)}, u32[]{:S(2)}, u32[]{:S(2)}) collective-permute-start(f32[3,1,8]{2,1,0:T(1,128)S(1)} %get-tuple-element.128), channel_id=1, source_target_pairs={{8,0},{16,8},{24,16},{32,24},{40,32},{48,40},{56,48},{9,1},{17,9},... | collective-permute-start | bytes 296 | tf_op jit(solution)/shard_map/ppermute | solution.py:23
  51.1 4.9 collective-permute-start.30
  72.8 4.2 collective-permute-start.4
  90.8 4.8 collective-permute-start.8
  95.7 4.3 collective-permute-start.18
  102.9 4.3 collective-permute-done.10
  114.0 4.3 collective-permute-start.12
  122.8 5.1 %collective-permute-start.20 = (f32[10,1,64]{2,1,0:T(1,128)S(1)}, f32[10,1,64]{2,1,0:T(1,128)S(1)}, u32[]{:S(2)}, u32[]{:S(2)}) collective-permute-start(f32[10,1,64]{2,1,0:T(1,128)S(1)} %get-tuple-element.63), channel_id=1, source_target_pairs={{0,8},{8,16},{16,24},{24,32},{32,40},{40,48},{48,56},{1,9},{9,17},... | collective-permute-start | bytes 7688 | tf_op jit(solution)/shard_map/ppermute | solution.py:21
  140.1 5.9 %collective-permute-done.16 = f32[18,34,1]{2,1,0:T(8,128)S(1)} collective-permute-done((f32[18,34,1]{2,1,0:T(8,128)S(1)}, f32[18,34,1]{2,1,0:T(8,128)S(1)}, u32[]{:S(2)}, u32[]{:S(2)}) %collective-permute-start.16) | collective-permute-done | bytes 2480 | tf_op jit(solution)/shard_map/ppermute | solution.py:21
  151.0 5.4 %collective-permute-start.22 = (f32[10,18,1]{2,1,0:T(8,128)S(1)}, f32[10,18,1]{2,1,0:T(8,128)S(1)}, u32[]{:S(2)}, u32[]{:S(2)}) collective-permute-start(f32[10,18,1]{2,1,0:T(8,128)S(1)} %get-tuple-element.57), channel_id=1, source_target_pairs={{0,1},{1,2},{2,3},{3,4},{4,5},{5,6},{6,7},{8,9},{9,10},{10,11},{11... | collective-permute-start | bytes 2168 | tf_op jit(solution)/shard_map/ppermute | solution.py:21
  157.1 18.2 %reshape.94 = f32[8,2,16,2,64,2]{5,4,3,2,1,0:T(8,128)} reshape(f32[16,32,128]{2,1,0:T(8,128)S(1)} %fusion.42) | data formatting | bytes 524288 | tf_op jit(solution)/shard_map/reshape | solution.py:32
  175.2 7.0 %reduce_sum.86 = f32[8,16,64]{2,1,0:T(8,128)S(1)} reduce(f32[8,2,16,2,64,2]{5,4,3,2,1,0:T(8,128)} %reshape.94, f32[]{:T(128)} %constant.14.clone.1), dimensions={1,3,5}, to_apply=%region_0.0 | reduce | flops 57344 | bytes 294916 | tf_op jit(solution)/shard_map/reduce_sum | solution.py:33
  190.2 4.9 collective-permute-start.26
  198.4 4.6 collective-permute-start.34
  224.3 7.1 %collective-permute-start.38 = (f32[6,1,32]{2,1,0:T(1,128)S(1)}, f32[6,1,32]{2,1,0:T(1,128)S(1)}, u32[]{:S(2)}, u32[]{:S(2)}) collective-permute-start(f32[6,1,32]{2,1,0:T(1,128)S(1)} %get-tuple-element.84), channel_id=1, source_target_pairs={{0,8},{8,16},{16,24},{24,32},{32,40},{40,48},{48,56},{1,9},{9,17},... | collective-permute-start | bytes 2312 | tf_op jit(solution)/shard_map/ppermute | solution.py:21
  242.8 4.9 collective-permute-start.46
  263.3 4.5 collective-permute-start.58
  284.5 6.2 %collective-permute-start.62 = (f32[3,1,8]{2,1,0:T(1,128)S(1)}, f32[3,1,8]{2,1,0:T(1,128)S(1)}, u32[]{:S(2)}, u32[]{:S(2)}) collective-permute-start(f32[3,1,8]{2,1,0:T(1,128)S(1)} %get-tuple-element.126), channel_id=1, source_target_pairs={{0,8},{8,16},{16,24},{24,32},{32,40},{40,48},{48,56},{1,9},{9,17},... | collective-permute-start | bytes 296 | tf_op jit(solution)/shard_map/ppermute | solution.py:21
  295.7 5.2 %collective-permute-start.64 = (f32[3,4,1]{2,1,0:T(4,128)S(1)}, f32[3,4,1]{2,1,0:T(4,128)S(1)}, u32[]{:S(2)}, u32[]{:S(2)}) collective-permute-start(f32[3,4,1]{2,1,0:T(4,128)S(1)} %get-tuple-element.110), channel_id=1, source_target_pairs={{0,1},{1,2},{2,3},{3,4},{4,5},{5,6},{6,7},{8,9},{9,10},{10,11},{11... | collective-permute-start | bytes 152 | tf_op jit(solution)/shard_map/ppermute | solution.py:21
  307.0 4.5 collective-permute-start.66
  321.2 4.8 collective-permute-start.70
  332.1 4.5 collective-permute-start.72
  363.1 4.5 collective-permute-start.80
  389.4 4.5 collective-permute-start.86
  416.8 4.8 collective-permute-start.92
  444.1 5.5 %collective-permute-start.98 = (f32[18,1,128]{2,1,0:T(1,128)S(1)}, f32[18,1,128]{2,1,0:T(1,128)S(1)}, u32[]{:S(2)}, u32[]{:S(2)}) collective-permute-start(f32[18,1,128]{2,1,0:T(1,128)S(1)} %get-tuple-element.34), channel_id=1, source_target_pairs={{0,8},{8,16},{16,24},{24,32},{32,40},{40,48},{48,56},{1,9},{9,17},... | collective-permute-start | bytes 27656 | tf_op jit(solution)/shard_map/ppermute | solution.py:21
  459.0 5.6 %collective-permute-done.100 = f32[18,34,1]{2,1,0:T(8,128)S(1)} collective-permute-done((f32[18,34,1]{2,1,0:T(8,128)S(1)}, f32[18,34,1]{2,1,0:T(8,128)S(1)}, u32[]{:S(2)}, u32[]{:S(2)}) %collective-permute-start.100) | collective-permute-done | bytes 2480 | tf_op jit(solution)/shard_map/ppermute | solution.py:21
  476.7 5.6 %collective-permute-start.104 = (f32[18,1,128]{2,1,0:T(1,128)S(1)}, f32[18,1,128]{2,1,0:T(1,128)S(1)}, u32[]{:S(2)}, u32[]{:S(2)}) collective-permute-start(f32[18,1,128]{2,1,0:T(1,128)S(1)} %get-tuple-element.32), channel_id=1, source_target_pairs={{0,8},{8,16},{16,24},{24,32},{32,40},{40,48},{48,56},{1,9},{9,17},... | collective-permute-start | bytes 27656 | tf_op jit(solution)/shard_map/ppermute | solution.py:21
  491.6 5.6 %collective-permute-done.106 = f32[18,34,1]{2,1,0:T(8,128)S(1)} collective-permute-done((f32[18,34,1]{2,1,0:T(8,128)S(1)}, f32[18,34,1]{2,1,0:T(8,128)S(1)}, u32[]{:S(2)}, u32[]{:S(2)}) %collective-permute-start.106) | collective-permute-done | bytes 2480 | tf_op jit(solution)/shard_map/ppermute | solution.py:21
  (409 shorter events, 307.7 us)
Async XLA Ops:
  29.5 12.6 %collective-permute-start.55 = (f32[1,2,8]{2,1,0:T(2,128)S(1)}, f32[1,2,8]{2,1,0:T(2,128)S(1)}, u32[]{:S(2)}, u32[]{:S(2)}) collective-permute-start(f32[1,2,8]{2,1,0:T(2,128)S(1)} %multiply_bitcast_fusion), channel_id=1, source_target_pairs={{64,0},{128,64},{192,128},{65,1},{129,65},{193,129},{66,2},{130,66... | collective-permute-start | bytes 200 | tf_op jit(solution)/shard_map/ppermute | solution.py:23
  30.8 11.4 %collective-permute-start.54 = (f32[1,2,8]{2,1,0:T(2,128)S(1)}, f32[1,2,8]{2,1,0:T(2,128)S(1)}, u32[]{:S(2)}, u32[]{:S(2)}) collective-permute-start(f32[1,2,8]{2,1,0:T(2,128)S(1)} %multiply_bitcast_fusion), channel_id=1, source_target_pairs={{0,64},{64,128},{128,192},{1,65},{65,129},{129,193},{2,66},{66,130... | collective-permute-start | bytes 200 | tf_op jit(solution)/shard_map/ppermute | solution.py:21
  35.5 41.5 %collective-permute-start.3 = (f32[1,32,128]{2,1,0:T(8,128)S(1)}, f32[1,32,128]{2,1,0:T(8,128)S(1)}, u32[]{:S(2)}, u32[]{:S(2)}) collective-permute-start(f32[1,32,128]{2,1,0:T(8,128)S(1)} %get-tuple-element.50), channel_id=1, source_target_pairs={{64,0},{128,64},{192,128},{65,1},{129,65},{193,129},{66,2},{130,66... | collective-permute-start | bytes 49160 | tf_op jit(solution)/shard_map/ppermute | solution.py:23
  36.8 40.1 %collective-permute-start.1 = (f32[1,32,128]{2,1,0:T(8,128)S(1)}, f32[1,32,128]{2,1,0:T(8,128)S(1)}, u32[]{:S(2)}, u32[]{:S(2)}) collective-permute-start(f32[1,32,128]{2,1,0:T(8,128)S(1)} %get-tuple-element.51), channel_id=1, source_target_pairs={{0,64},{64,128},{128,192},{1,65},{65,129},{129,193},{2,66},{66,130... | collective-permute-start | bytes 49160 | tf_op jit(solution)/shard_map/ppermute | solution.py:21
  40.9 29.9 %collective-permute-start.2 = (f32[1,32,128]{2,1,0:T(8,128)S(1)}, f32[1,32,128]{2,1,0:T(8,128)S(1)}, u32[]{:S(2)}, u32[]{:S(2)}) collective-permute-start(f32[1,32,128]{2,1,0:T(8,128)S(1)} %get-tuple-element.48), channel_id=1, source_target_pairs={{64,0},{128,64},{192,128},{65,1},{129,65},{193,129},{66,2},{130,66... | collective-permute-start | bytes 49160 | tf_op jit(solution)/shard_map/ppermute | solution.py:23
  62.0 8.7 %collective-permute-start = (f32[1,32,128]{2,1,0:T(8,128)S(1)}, f32[1,32,128]{2,1,0:T(8,128)S(1)}, u32[]{:S(2)}, u32[]{:S(2)}) collective-permute-start(f32[1,32,128]{2,1,0:T(8,128)S(1)} %get-tuple-element.49), channel_id=1, source_target_pairs={{0,64},{64,128},{128,192},{1,65},{65,129},{129,193},{2,66},{66,130... | collective-permute-start | bytes 49160 | tf_op jit(solution)/shard_map/ppermute | solution.py:21
  69.4 44.6 %collective-permute-start.19 = (f32[1,16,64]{2,1,0:T(8,128)S(1)}, f32[1,16,64]{2,1,0:T(8,128)S(1)}, u32[]{:S(2)}, u32[]{:S(2)}) collective-permute-start(f32[1,16,64]{2,1,0:T(8,128)S(1)} %get-tuple-element.68), channel_id=1, source_target_pairs={{64,0},{128,64},{192,128},{65,1},{129,65},{193,129},{66,2},{130,66... | collective-permute-start | bytes 12296 | tf_op jit(solution)/shard_map/ppermute | solution.py:23
  70.8 10.6 %collective-permute-start.6 = (f32[18,1,128]{2,1,0:T(1,128)S(1)}, f32[18,1,128]{2,1,0:T(1,128)S(1)}, u32[]{:S(2)}, u32[]{:S(2)}) collective-permute-start(f32[18,1,128]{2,1,0:T(1,128)S(1)} %get-tuple-element.38), channel_id=1, source_target_pairs={{8,0},{16,8},{24,16},{32,24},{40,32},{48,40},{56,48},{9,1},{17,9},... | collective-permute-start | bytes 27656 | tf_op jit(solution)/shard_map/ppermute | solution.py:23
  72.8 8.6 %collective-permute-start.4 = (f32[18,1,128]{2,1,0:T(1,128)S(1)}, f32[18,1,128]{2,1,0:T(1,128)S(1)}, u32[]{:S(2)}, u32[]{:S(2)}) collective-permute-start(f32[18,1,128]{2,1,0:T(1,128)S(1)} %get-tuple-element.39), channel_id=1, source_target_pairs={{0,8},{8,16},{16,24},{24,32},{32,40},{40,48},{48,56},{1,9},{9,17},... | collective-permute-start | bytes 27656 | tf_op jit(solution)/shard_map/ppermute | solution.py:21
  84.7 11.0 %collective-permute-start.9 = (f32[18,34,1]{2,1,0:T(8,128)S(1)}, f32[18,34,1]{2,1,0:T(8,128)S(1)}, u32[]{:S(2)}, u32[]{:S(2)}) collective-permute-start(f32[18,34,1]{2,1,0:T(8,128)S(1)} %get-tuple-element.30), channel_id=1, source_target_pairs={{0,1},{1,2},{2,3},{3,4},{4,5},{5,6},{6,7},{8,9},{9,10},{10,11},{11... | collective-permute-start | bytes 7352 | tf_op jit(solution)/shard_map/ppermute | solution.py:21
  88.2 12.7 %collective-permute-start.11 = (f32[18,34,1]{2,1,0:T(8,128)S(1)}, f32[18,34,1]{2,1,0:T(8,128)S(1)}, u32[]{:S(2)}, u32[]{:S(2)}) collective-permute-start(f32[18,34,1]{2,1,0:T(8,128)S(1)} %get-tuple-element.31), channel_id=1, source_target_pairs={{1,0},{2,1},{3,2},{4,3},{5,4},{6,5},{7,6},{9,8},{10,9},{11,10},{12... | collective-permute-start | bytes 7352 | tf_op jit(solution)/shard_map/ppermute | solution.py:23
  89.5 17.6 %collective-permute-start.10 = (f32[18,34,1]{2,1,0:T(8,128)S(1)}, f32[18,34,1]{2,1,0:T(8,128)S(1)}, u32[]{:S(2)}, u32[]{:S(2)}) collective-permute-start(f32[18,34,1]{2,1,0:T(8,128)S(1)} %get-tuple-element.28), channel_id=1, source_target_pairs={{1,0},{2,1},{3,2},{4,3},{5,4},{6,5},{7,6},{9,8},{10,9},{11,10},{12... | collective-permute-start | bytes 7352 | tf_op jit(solution)/shard_map/ppermute | solution.py:23
  90.8 20.5 %collective-permute-start.8 = (f32[18,34,1]{2,1,0:T(8,128)S(1)}, f32[18,34,1]{2,1,0:T(8,128)S(1)}, u32[]{:S(2)}, u32[]{:S(2)}) collective-permute-start(f32[18,34,1]{2,1,0:T(8,128)S(1)} %get-tuple-element.29), channel_id=1, source_target_pairs={{0,1},{1,2},{2,3},{3,4},{4,5},{5,6},{6,7},{8,9},{9,10},{10,11},{11... | collective-permute-start | bytes 7352 | tf_op jit(solution)/shard_map/ppermute | solution.py:21
  95.7 22.6 %collective-permute-start.18 = (f32[1,16,64]{2,1,0:T(8,128)S(1)}, f32[1,16,64]{2,1,0:T(8,128)S(1)}, u32[]{:S(2)}, u32[]{:S(2)}) collective-permute-start(f32[1,16,64]{2,1,0:T(8,128)S(1)} %get-tuple-element.69), channel_id=1, source_target_pairs={{0,64},{64,128},{128,192},{1,65},{65,129},{129,193},{2,66},{66,130... | collective-permute-start | bytes 12296 | tf_op jit(solution)/shard_map/ppermute | solution.py:21
  101.0 120.3 %collective-permute-start.45 = (f32[4,1,16]{2,1,0:T(1,128)}, f32[4,1,16]{2,1,0:T(1,128)}, u32[]{:S(2)}, u32[]{:S(2)}) collective-permute-start(f32[4,1,16]{2,1,0:T(1,128)} %get-tuple-element.104), channel_id=1, source_target_pairs={{8,0},{16,8},{24,16},{32,24},{40,32},{48,40},{56,48},{9,1},{17,9},... | collective-permute-start | bytes 776 | tf_op jit(solution)/shard_map/ppermute | solution.py:23
  107.2 114.1 %collective-permute-start.44 = (f32[4,1,16]{2,1,0:T(1,128)}, f32[4,1,16]{2,1,0:T(1,128)}, u32[]{:S(2)}, u32[]{:S(2)}) collective-permute-start(f32[4,1,16]{2,1,0:T(1,128)} %get-tuple-element.105), channel_id=1, source_target_pairs={{0,8},{8,16},{16,24},{24,32},{32,40},{40,48},{48,56},{1,9},{9,17},... | collective-permute-start | bytes 776 | tf_op jit(solution)/shard_map/ppermute | solution.py:21
  111.3 75.9 %collective-permute-start.33 = (f32[6,1,32]{2,1,0:T(1,128)S(1)}, f32[6,1,32]{2,1,0:T(1,128)S(1)}, u32[]{:S(2)}, u32[]{:S(2)}) collective-permute-start(f32[6,1,32]{2,1,0:T(1,128)S(1)} %get-tuple-element.86), channel_id=1, source_target_pairs={{8,0},{16,8},{24,16},{32,24},{40,32},{48,40},{56,48},{9,1},{17,9},... | collective-permute-start | bytes 2312 | tf_op jit(solution)/shard_map/ppermute | solution.py:23
  135.2 10.9 %collective-permute-start.16 = (f32[18,34,1]{2,1,0:T(8,128)S(1)}, f32[18,34,1]{2,1,0:T(8,128)S(1)}, u32[]{:S(2)}, u32[]{:S(2)}) collective-permute-start(f32[18,34,1]{2,1,0:T(8,128)S(1)} %get-tuple-element.26), channel_id=1, source_target_pairs={{0,1},{1,2},{2,3},{3,4},{4,5},{5,6},{6,7},{8,9},{9,10},{10,11},{11... | collective-permute-start | bytes 7352 | tf_op jit(solution)/shard_map/ppermute | solution.py:21
  138.7 12.3 %collective-permute-start.17 = (f32[18,34,1]{2,1,0:T(8,128)S(1)}, f32[18,34,1]{2,1,0:T(8,128)S(1)}, u32[]{:S(2)}, u32[]{:S(2)}) collective-permute-start(f32[18,34,1]{2,1,0:T(8,128)S(1)} %get-tuple-element.27), channel_id=1, source_target_pairs={{1,0},{2,1},{3,2},{4,3},{5,4},{6,5},{7,6},{9,8},{10,9},{11,10},{12... | collective-permute-start | bytes 7352 | tf_op jit(solution)/shard_map/ppermute | solution.py:23
  146.0 36.3 %collective-permute-start.23 = (f32[10,18,1]{2,1,0:T(8,128)S(1)}, f32[10,18,1]{2,1,0:T(8,128)S(1)}, u32[]{:S(2)}, u32[]{:S(2)}) collective-permute-start(f32[10,18,1]{2,1,0:T(8,128)S(1)} %get-tuple-element.56), channel_id=1, source_target_pairs={{1,0},{2,1},{3,2},{4,3},{5,4},{6,5},{7,6},{9,8},{10,9},{11,10},{12... | collective-permute-start | bytes 2168 | tf_op jit(solution)/shard_map/ppermute | solution.py:23
  151.0 31.3 %collective-permute-start.22 = (f32[10,18,1]{2,1,0:T(8,128)S(1)}, f32[10,18,1]{2,1,0:T(8,128)S(1)}, u32[]{:S(2)}, u32[]{:S(2)}) collective-permute-start(f32[10,18,1]{2,1,0:T(8,128)S(1)} %get-tuple-element.57), channel_id=1, source_target_pairs={{0,1},{1,2},{2,3},{3,4},{4,5},{5,6},{6,7},{8,9},{9,10},{10,11},{11... | collective-permute-start | bytes 2168 | tf_op jit(solution)/shard_map/ppermute | solution.py:21
  197.1 9.4 %collective-permute-start.35 = (f32[6,10,1]{2,0,1:T(8,128)S(1)}, f32[6,10,1]{2,0,1:T(8,128)S(1)}, u32[]{:S(2)}, u32[]{:S(2)}) collective-permute-start(f32[6,10,1]{2,0,1:T(8,128)S(1)} %get-tuple-element.80), channel_id=1, source_target_pairs={{1,0},{2,1},{3,2},{4,3},{5,4},{6,5},{7,6},{9,8},{10,9},{11,10},{12... | collective-permute-start | bytes 728 | tf_op jit(solution)/shard_map/ppermute | solution.py:23
  198.4 9.4 %collective-permute-start.34 = (f32[6,10,1]{2,0,1:T(8,128)S(1)}, f32[6,10,1]{2,0,1:T(8,128)S(1)}, u32[]{:S(2)}, u32[]{:S(2)}) collective-permute-start(f32[6,10,1]{2,0,1:T(8,128)S(1)} %get-tuple-element.81), channel_id=1, source_target_pairs={{0,1},{1,2},{2,3},{3,4},{4,5},{5,6},{6,7},{8,9},{9,10},{10,11},{11... | collective-permute-start | bytes 728 | tf_op jit(solution)/shard_map/ppermute | solution.py:21
  224.3 9.1 %collective-permute-start.38 = (f32[6,1,32]{2,1,0:T(1,128)S(1)}, f32[6,1,32]{2,1,0:T(1,128)S(1)}, u32[]{:S(2)}, u32[]{:S(2)}) collective-permute-start(f32[6,1,32]{2,1,0:T(1,128)S(1)} %get-tuple-element.84), channel_id=1, source_target_pairs={{0,8},{8,16},{16,24},{24,32},{32,40},{40,48},{48,56},{1,9},{9,17},... | collective-permute-start | bytes 2312 | tf_op jit(solution)/shard_map/ppermute | solution.py:21
  236.5 11.2 %collective-permute-start.40 = (f32[6,10,1]{2,0,1:T(8,128)S(1)}, f32[6,10,1]{2,0,1:T(8,128)S(1)}, u32[]{:S(2)}, u32[]{:S(2)}) collective-permute-start(f32[6,10,1]{2,0,1:T(8,128)S(1)} %get-tuple-element.76), channel_id=1, source_target_pairs={{0,1},{1,2},{2,3},{3,4},{4,5},{5,6},{6,7},{8,9},{9,10},{10,11},{11... | collective-permute-start | bytes 728 | tf_op jit(solution)/shard_map/ppermute | solution.py:21
  256.1 11.8 %collective-permute-start.50 = (f32[4,1,16]{2,1,0:T(1,128)S(1)}, f32[4,1,16]{2,1,0:T(1,128)S(1)}, u32[]{:S(2)}, u32[]{:S(2)}) collective-permute-start(f32[4,1,16]{2,1,0:T(1,128)S(1)} %get-tuple-element.102), channel_id=1, source_target_pairs={{0,8},{8,16},{16,24},{24,32},{32,40},{40,48},{48,56},{1,9},{9,17},... | collective-permute-start | bytes 776 | tf_op jit(solution)/shard_map/ppermute | solution.py:21
  262.0 15.5 %collective-permute-start.59 = (f32[3,4,1]{2,1,0:T(4,128)S(1)}, f32[3,4,1]{2,1,0:T(4,128)S(1)}, u32[]{:S(2)}, u32[]{:S(2)}) collective-permute-start(f32[3,4,1]{2,1,0:T(4,128)S(1)} %get-tuple-element.112), channel_id=1, source_target_pairs={{1,0},{2,1},{3,2},{4,3},{5,4},{6,5},{7,6},{9,8},{10,9},{11,10},{12... | collective-permute-start | bytes 152 | tf_op jit(solution)/shard_map/ppermute | solution.py:23
  263.3 14.2 %collective-permute-start.58 = (f32[3,4,1]{2,1,0:T(4,128)S(1)}, f32[3,4,1]{2,1,0:T(4,128)S(1)}, u32[]{:S(2)}, u32[]{:S(2)}) collective-permute-start(f32[3,4,1]{2,1,0:T(4,128)S(1)} %get-tuple-element.113), channel_id=1, source_target_pairs={{0,1},{1,2},{2,3},{3,4},{4,5},{5,6},{6,7},{8,9},{9,10},{10,11},{11... | collective-permute-start | bytes 152 | tf_op jit(solution)/shard_map/ppermute | solution.py:21
  454.8 9.8 %collective-permute-start.100 = (f32[18,34,1]{2,1,0:T(8,128)S(1)}, f32[18,34,1]{2,1,0:T(8,128)S(1)}, u32[]{:S(2)}, u32[]{:S(2)}) collective-permute-start(f32[18,34,1]{2,1,0:T(8,128)S(1)} %get-tuple-element.24), channel_id=1, source_target_pairs={{0,1},{1,2},{2,3},{3,4},{4,5},{5,6},{6,7},{8,9},{9,10},{10,11},{11... | collective-permute-start | bytes 7352 | tf_op jit(solution)/shard_map/ppermute | solution.py:21
  457.7 11.0 %collective-permute-start.101 = (f32[18,34,1]{2,1,0:T(8,128)S(1)}, f32[18,34,1]{2,1,0:T(8,128)S(1)}, u32[]{:S(2)}, u32[]{:S(2)}) collective-permute-start(f32[18,34,1]{2,1,0:T(8,128)S(1)} %get-tuple-element.25), channel_id=1, source_target_pairs={{1,0},{2,1},{3,2},{4,3},{5,4},{6,5},{7,6},{9,8},{10,9},{11,10},{12... | collective-permute-start | bytes 7352 | tf_op jit(solution)/shard_map/ppermute | solution.py:23
  487.5 9.8 %collective-permute-start.106 = (f32[18,34,1]{2,1,0:T(8,128)S(1)}, f32[18,34,1]{2,1,0:T(8,128)S(1)}, u32[]{:S(2)}, u32[]{:S(2)}) collective-permute-start(f32[18,34,1]{2,1,0:T(8,128)S(1)} %get-tuple-element.22), channel_id=1, source_target_pairs={{0,1},{1,2},{2,3},{3,4},{4,5},{5,6},{6,7},{8,9},{9,10},{10,11},{11... | collective-permute-start | bytes 7352 | tf_op jit(solution)/shard_map/ppermute | solution.py:21
  490.3 11.0 %collective-permute-start.107 = (f32[18,34,1]{2,1,0:T(8,128)S(1)}, f32[18,34,1]{2,1,0:T(8,128)S(1)}, u32[]{:S(2)}, u32[]{:S(2)}) collective-permute-start(f32[18,34,1]{2,1,0:T(8,128)S(1)} %get-tuple-element.23), channel_id=1, source_target_pairs={{1,0},{2,1},{3,2},{4,3},{5,4},{6,5},{7,6},{9,8},{10,9},{11,10},{12... | collective-permute-start | bytes 7352 | tf_op jit(solution)/shard_map/ppermute | solution.py:23
  (112 other events, 4031.5 us)
where the time goes:
time: 506 us; the launch traced here: 503 us
  starting transfers between devices  297 us (59%)
  waiting for transfers between devices  122 us (24%)
  local copies, waits for them, and re-layouts  47.3 us (9%)
  other arithmetic  33.6 us (7%)
    ppermute x54, starting transfers between devices, extended(): lax.ppermute(tail, axis, [(i, (i + 1) % count) for i in range(ends)])  212 us
    ppermute x54, waiting for transfers between devices, extended(): lax.ppermute(head, axis, [((i + 1) % count, i) for i in range(ends)])  102 us
    ppermute x54, starting transfers between devices, extended(): lax.ppermute(head, axis, [((i + 1) % count, i) for i in range(ends)])  85.4 us
    reshape x4, local copies, waits for them, and re-layouts, coarsen(): values.reshape(span_first // 2, 2, span_second // 2, 2, span_third // 2, 2)  40.2 us
    ppermute x54, waiting for transfers between devices, extended(): lax.ppermute(tail, axis, [(i, (i + 1) % count) for i in range(ends)])  20.1 us
    reduce_sum x10, other arithmetic, coarsen(): return jnp.mean(blocks, axis=(1, 3, 5))  16.3 us
  transfers between devices with their start and end apart: 108, of which 41 were waited for; matrix products, arithmetic and copies ran while one was open for 8% of the time, Pallas kernels for 0%

commit v1 on v0

v1 whole, which is shorter than its diff:
```python
import functools

import jax
import jax.numpy as jnp
from jax import lax
from jax.experimental import pallas as pl
from jax.experimental.pallas import tpu as pltpu
from jax.sharding import PartitionSpec as P

OMEGA = 0.8
MESH = pl.DeviceIdType.MESH
F32 = jnp.float32

X0, Y0, LANES = 16, 32, 128
X1, Y1 = 8, 16
X2, Y2, Z2 = 4, 8, 32
REACH = 3
ROWS = (2 * REACH + 1) * Y2
OWN = REACH * Y2


def iota(shape, dim):
    return lax.broadcasted_iota(jnp.int32, shape, dim)


def roll(v, shift, axis):
    size = v.shape[axis]
    if isinstance(shift, int):
        shift = shift % size
        if shift == 0:
            return v
    return pltpu.roll(v, shift, axis=axis)


def loop(count, body, init=0, unroll=True):
    return lax.fori_loop(0, count, body, init, unroll=unroll)


class Faces:
    def __init__(self, net, field, sent, got, nx, ny):
        self.net = net
        self.copies = {}
        lead = (slice(None),) * (len(field.shape) - 3)
        for d in (-1, 1):
            src, dst = (1, nx + 1) if d < 0 else (nx, 0)
            self.copies[(d, 0, 0)] = net.copy(
                field.at[lead + (src, pl.ds(8, ny))], field.at[lead + (dst, pl.ds(8, ny))], (d, 0, 0)
            )
            src, dst = (8, 8 + ny) if d < 0 else (7 + ny, 7)
            self.copies[(0, d, 0)] = net.copy(
                field.at[lead + (pl.ds(1, nx), pl.ds(src, 1))],
                field.at[lead + (pl.ds(1, nx), pl.ds(dst, 1))],
                (0, d, 0),
            )
            self.copies[(0, 0, d)] = net.copy(sent, got.at[0 if d > 0 else 1], (0, 0, d))

    def start(self):
        for way in ((0, 0, 1), (0, 0, -1), (1, 0, 0), (-1, 0, 0), (0, 1, 0), (0, -1, 0)):
            self.net.start(self.copies[way])

    def wait(self):
        for copy in self.copies.values():
            self.net.wait_recv(copy)


class Net:
    def __init__(self, sizes, send_sems, recv_sems):
        self.me = tuple(lax.axis_index(a) for a in ("gx", "gy", "gz"))
        self.sizes = sizes
        self.send_sems, self.recv_sems = send_sems, recv_sems
        self.used = 0
        self.started = []

    def there(self, way):
        found = None
        for at, size, d in zip(self.me, self.sizes, way):
            if d:
                ok = (at + d < size) if d > 0 else (at + d >= 0)
                found = ok if found is None else jnp.logical_and(found, ok)
        return found

    def when(self, way):
        found = self.there(way)
        return (lambda f: f()) if found is None else pl.when(found)

    def device(self, way, turn=0):
        x = self.me[0] + way[0]
        if turn:
            x = lax.rem(x + turn, self.sizes[0])
        return (x, self.me[1] + way[1], self.me[2] + way[2])

    def copy(self, src, dst, way, turn=0):
        i = self.used
        self.used += 1
        made = pltpu.make_async_remote_copy(
            src_ref=src,
            dst_ref=dst,
            send_sem=self.send_sems.at[i],
            recv_sem=self.recv_sems.at[i],
            device_id=self.device(way, turn),
            device_id_type=MESH,
        )
        return (made, way)

    def start(self, copy):
        made, way = copy
        self.started.append(copy)

        @self.when(way)
        def _():
            made.start()

    def wait_recv(self, copy):
        made, way = copy

        @self.when(tuple(-d for d in way))
        def _():
            made.wait_recv()

    def finish(self):
        for made, way in self.started:

            @self.when(way)
            def _():
                made.wait_send()


SEMS = 80


def pack_z(acc, v, first, w):
    group = iota((8, LANES), 1) // (2 * w)
    for j in range(v.shape[0] // 8):
        k = first + j
        acc = jnp.where(group == k, roll(v[8 * j : 8 * j + 8], (2 * k + 1) * w, 1), acc)
    return acc


def merge_z(got, w):
    return jnp.where((iota((8, LANES), 1) // w) % 2 == 0, got[0], got[1])


def unpack_z(both, first, tiles, w):
    return jnp.concatenate([roll(both, LANES - (2 * (first + j) + 1) * w, 1) for j in range(tiles)], axis=0)


def z_sides(v, halo, w):
    lane = iota(v.shape, 1)
    below = roll(jnp.where(lane >= LANES - w, halo, v), w, 1)
    above = roll(jnp.where(lane < w, halo, v), LANES - w, 1)
    return below, above


def sides(field, x, rows, first, step, below, above, lead=()):
    f = lambda dx, dy: field[lead + (x + 1 + dx, pl.ds(first + dy, rows))]
    return (f(-1, 0), f(1, 0), f(0, -step), f(0, step), below, above)


def weighted(cs, vs):
    total = cs[0] * vs[0]
    for c, v in zip(cs[1:], vs[1:]):
        total = total + c * v
    return total


def pair_sum(v, step, axis):
    even = (iota(v.shape, axis) // step) % 2 == 0
    size = v.shape[axis]
    return v + jnp.where(even, roll(v, size - step, axis), roll(v, step, axis))


def kernel(
    sizes,
    rhs_hbm, permit_hbm, guess_hbm,
    sol_hbm, res_hbm,
    rhs, gp, smooth, v0, sol, res, st0, zs0, zr0,
    p1, u1, v1, rw1, b1, st1, tmp, hw1, rw0, zs1, zr1, pick, spread,
    raw_p, raw_b, p2, u2, b2, st2, p3, u3, v3, b3, st3, p4, wa, wb, b4, st4, w3, v2, w2,
    local_sems, send_sems, recv_sems,
):
    nx = sizes[0]
    net = Net(sizes, send_sems, recv_sems)
    ix, iy, iz = net.me
    inner0 = (pl.ds(1, X0), pl.ds(8, Y0))

    loads = [
        pltpu.make_async_copy(guess_hbm, gp.at[(0,) + inner0], local_sems.at[0]),
        pltpu.make_async_copy(permit_hbm, gp.at[(1,) + inner0], local_sems.at[1]),
        pltpu.make_async_copy(rhs_hbm, rhs, local_sems.at[2]),
    ]
    for load in loads:
        load.start()

    ways = [(0, 0, 1), (0, 0, -1), (1, 0, 0), (-1, 0, 0), (0, 1, 0), (0, -1, 0)]
    barrier = pltpu.get_barrier_semaphore()
    for way in ways:

        @net.when(way)
        def _():
            pl.semaphore_signal(barrier, inc=1, device_id=net.device(way), device_id_type=MESH)

    fields0 = [(gp.at[0], X0, Y0), (gp.at[1], X0, Y0), (smooth, X0, Y0), (v0, X0, Y0), (sol, X0, Y0)]
    fields1 = [(p1, X1, Y1), (u1, X1, Y1)]

    def clear(fields, zr):
        for way in ways:
            out = net.there(way)

            @pl.when(jnp.logical_not(out))
            def _():
                side = sum(way) > 0
                for f, fx, fy in fields:
                    if way[0]:
                        f[fx + 1 if side else 0] = jnp.zeros((fy + 16, LANES), F32)
                    elif way[1]:
                        at = 8 + fy if side else 7
                        f[pl.ds(1, fx), pl.ds(at, 1)] = jnp.zeros((fx, 1, LANES), F32)
                if way[2]:
                    for r in range(zr.shape[0]):
                        zr[r, 1 if side else 0] = jnp.zeros(zr.shape[2:], F32)

    clear(fields0, zr0)

    loads[0].wait()
    loads[1].wait()

    def pack_gp(x, accs):
        return tuple(pack_z(a, gp[i, x + 1, 8 : 8 + Y0], 4 * x, 1) for i, a in enumerate(accs))

    zero = jnp.zeros((8, LANES), F32)
    accs = loop(X0, pack_gp, (zero, zero))
    zs0[0, :8] = accs[0]
    zs0[0, 8:] = accs[1]

    pl.semaphore_wait(barrier, sum(net.there(way).astype(jnp.int32) for way in ways))

    round_a = Faces(net, gp, zs0.at[0], zr0.at[0], X0, Y0)
    round_a.start()

    def coarse_p1(x, acc):
        tmp[x] = gp[1, 2 * x + 1, 8 : 8 + Y0] + gp[1, 2 * x + 2, 8 : 8 + Y0]
        v = tmp[x, pl.ds(0, Y1, stride=2)] + tmp[x, pl.ds(1, Y1, stride=2)]
        v = 0.125 * pair_sum(v, 1, 1)
        p1[x + 1, 8 : 8 + Y1] = v
        return pack_z(acc, v, 2 * x, 2)

    clear(fields1, zr1)
    zs1[0] = loop(X1, coarse_p1, zero)
    faces_p1 = Faces(net, p1, zs1.at[0], zr1.at[0], X1, Y1)
    faces_p1.start()

    for x in range(X2):
        row, col = iota((LANES, LANES), 0), iota((LANES, LANES), 1)
        take = jnp.logical_and(col == Z2 * x + row // 4, row % 2 == 0)
        pick[pl.ds(x * LANES, LANES)] = jnp.where(take, 0.125, 0.0).astype(F32)
    row, col = iota((LANES, LANES), 0), iota((LANES, LANES), 1)
    spread[:, :LANES] = (row == Z2 + col // 4).astype(F32)
    left = jnp.logical_and(row == Z2 - 1, col >= LANES - 2)
    right = jnp.logical_and(row == 2 * Z2, col < 2)
    spread[:, LANES:] = jnp.logical_or(left, right).astype(F32)

    def compact(planes):
        parts = []
        for x in range(X2):
            tmp[x, :Y1] = planes(2 * x) + planes(2 * x + 1)
            parts.append(tmp[x, pl.ds(0, Y2, stride=2)] + tmp[x, pl.ds(1, Y2, stride=2)])
        return lax.dot_general(
            jnp.concatenate(parts, axis=1), pick[...], (((1,), (0,)), ((), ())),
            precision=lax.Precision.HIGHEST, preferred_element_type=F32,
        )

    for raw in (raw_p, raw_b):
        for yd in range(2 * REACH + 1):
            if yd != REACH:
                d = yd - REACH

                @pl.when(jnp.logical_not(net.there((0, d, 0))))
                def _():
                    raw[yd] = jnp.zeros(raw.shape[1:], F32)

        for zd in (0, 2):

            @pl.when(jnp.logical_not(net.there((0, 0, zd - 1))))
            def _():
                if raw is raw_p:
                    raw[REACH, ix, zd] = jnp.zeros((8, LANES), F32)
                else:
                    raw[REACH, :, zd] = jnp.zeros((nx, 8, LANES), F32)

    raw_p[REACH, ix, 1] = compact(lambda x: p1[x + 1, 8 : 8 + Y1])
    p2_z = [net.copy(raw_p.at[REACH, ix, 1], raw_p.at[REACH, ix, 1 - d], (0, 0, d)) for d in (1, -1)]
    for copy in p2_z:
        net.start(copy)
    loads[2].wait()

    def couplings(scale, p, ns):
        cs = [scale * (p + n) for n in ns]
        return cs, cs[0] + cs[1] + cs[2] + cs[3] + cs[4] + cs[5]

    round_a.wait()
    both_g = merge_z([zr0[0, 0, :8], zr0[0, 1, :8]], 1)
    both_p = merge_z([zr0[0, 0, 8:], zr0[0, 1, 8:]], 1)

    def stencil_sides0(field, x, both, lead=()):
        v = field[lead + (x + 1, pl.ds(8, Y0))]
        return v, sides(field, x, Y0, 8, 1, *z_sides(v, unpack_z(both, 4 * x, 4, 1), 1), lead=lead)

    def first(x, acc):
        p, ns = stencil_sides0(gp, x, both_p, (1,))
        cs, diag = couplings(0.5, p, ns)
        for i, c in enumerate(cs):
            st0[i, x] = c
        inv = OMEGA / diag
        st0[6, x] = diag
        st0[7, x] = inv
        v, vs = stencil_sides0(gp, x, both_g, (0,))
        s = (1.0 - OMEGA) * v + inv * (rhs[x] + weighted(cs, vs))
        smooth[x + 1, 8 : 8 + Y0] = s
        return pack_z(acc, s, 4 * x, 1)

    zs0[1, :8] = loop(X0, first, zero)

    def faces0(field, r):
        return Faces(net, field, zs0.at[r, pl.ds(0, 8)], zr0.at[r, :, pl.ds(0, 8)], X0, Y0)

    round_b = faces0(smooth, 1)
    round_b.start()

    faces_p1.wait()
    both_p1 = merge_z(zr1[0], 2)

    def sides1(field, x, halo):
        v = field[x + 1, 8 : 8 + Y1]
        return v, sides(field, x, Y1, 8, 1, *z_sides(v, halo, 2))

    def couple1(x, _):
        p, ns = sides1(p1, x, unpack_z(both_p1, 2 * x, 2, 2))
        cs, diag = couplings(0.125, p, ns)
        for i, c in enumerate(cs):
            st1[i, x] = c
        st1[6, x] = diag
        st1[7, x] = OMEGA / diag
        return 0

    loop(X1, couple1)

    round_b.wait()
    both_s = merge_z([zr0[1, 0, :8], zr0[1, 1, :8]], 1)

    def remainder0(field, x, both):
        v, vs = stencil_sides0(field, x, both)
        return rhs[x] - st0[6, x] * v + weighted([st0[i, x] for i in range(6)], vs)

    def down0(x, acc):
        tmp[x] = remainder0(smooth, 2 * x, both_s) + remainder0(smooth, 2 * x + 1, both_s)
        b = tmp[x, pl.ds(0, Y1, stride=2)] + tmp[x, pl.ds(1, Y1, stride=2)]
        b = 0.125 * pair_sum(b, 1, 1)
        b1[x] = b
        u = st1[7, x] * b
        u1[x + 1, 8 : 8 + Y1] = u
        return pack_z(acc, u, 2 * x, 2)

    zs1[1] = loop(X1, down0, zero)

    round_c = Faces(net, u1, zs1.at[1], zr1.at[1], X1, Y1)
    round_c.start()

    for copy in p2_z:
        net.wait_recv(copy)
    p2_x = [net.copy(raw_p.at[REACH, ix], raw_p.at[REACH, ix], (0, 0, 0), k) for k in range(1, nx)]
    for copy in p2_x:
        net.start(copy)

    round_c.wait()
    both_u = merge_z(zr1[1], 2)

    def remainder1(x):
        u, us = sides1(u1, x, unpack_z(both_u, 2 * x, 2, 2))
        return b1[x] - st1[6, x] * u + weighted([st1[i, x] for i in range(6)], us)

    raw_b[REACH, ix, 1] = compact(remainder1)

    mine = raw_b.at[REACH, ix, 1]
    b2_xz = []
    for d in (1, -1, 0):
        for k in range(nx):
            if d or k:
                b2_xz.append(net.copy(mine, raw_b.at[REACH, ix, 1 - d], (0, 0, d), k))
    for copy in b2_xz:
        net.start(copy)

    for copy in p2_x:
        net.wait_recv(copy)
    steps = [d for k in range(1, REACH + 1) for d in (k, -k)]
    p2_y = [net.copy(raw_p.at[REACH], raw_p.at[REACH - d], (0, d, 0)) for d in steps]
    for copy in p2_y:
        net.start(copy)

    for copy in b2_xz:
        net.wait_recv(copy)
    b2_y = [net.copy(raw_b.at[REACH], raw_b.at[REACH - d], (0, d, 0)) for d in steps]
    for copy in b2_y:
        net.start(copy)

    for f in (p2, u2, p3, u3, v3, p4, wa, wb):
        n = f.shape[0]
        f[0] = jnp.zeros(f.shape[1:], F32)
        f[n - 1] = jnp.zeros(f.shape[1:], F32)

        def pad(x, _):
            f[x, :8] = jnp.zeros((8, LANES), F32)
            f[x, 8 + ROWS :] = jnp.zeros((8, LANES), F32)
            return 0

        loop(n, pad)
    for f in (v2, w2):
        loop(f.shape[0], lambda x, _: f.__setitem__(x, jnp.zeros(f.shape[1:], F32)) or 0)

    def region(raw, xd, x):
        lane = iota((ROWS, LANES), 1)
        part = [
            roll(raw[:, xd, zd].reshape(ROWS, LANES), Z2 * (zd - x), 1) for zd in range(3)
        ]
        return jnp.where(lane < Z2, part[0], jnp.where(lane < 2 * Z2, part[1], jnp.where(lane < 3 * Z2, part[2], 0.0)))

    for copy in p2_y:
        net.wait_recv(copy)

    def unpack_p(xd, _):
        for x in range(X2):
            p2[X2 * xd + x + 1, 8 : 8 + ROWS] = region(raw_p, xd, x)
        return 0

    loop(nx, unpack_p)

    def coarse(v, step):
        return 0.125 * pair_sum(pair_sum(v, step, 0), step, 1)

    def coarse_p(src, dst, step):
        def one(x, _):
            v = src[2 * x + 1, 8 : 8 + ROWS] + src[2 * x + 2, 8 : 8 + ROWS]
            dst[x + 1, 8 : 8 + ROWS] = coarse(v, step)
            return 0

        loop(dst.shape[0] - 2, one)

    coarse_p(p2, p3, 1)
    coarse_p(p3, p4, 2)

    def region_sides(field, x, step, first=8, rows=ROWS):
        v = field[x + 1, pl.ds(first, rows)]
        return v, sides(field, x, rows, first, step, roll(v, step, 1), roll(v, LANES - step, 1))

    def couple_region(p_ref, st, step, scale):
        def one(x, _):
            p, ns = region_sides(p_ref, x, step)
            cs, diag = couplings(scale, p, ns)
            for i, c in enumerate(cs):
                st[i, x] = c
            inside = p > 0.0
            st[6, x] = diag
            st[7, x] = jnp.where(inside, OMEGA / jnp.where(inside, diag, 1.0), 0.0)
            return 0

        loop(p_ref.shape[0] - 2, one)

    couple_region(p2, st2, 1, 0.5 / 16)
    couple_region(p3, st3, 2, 0.5 / 64)
    couple_region(p4, st4, 4, 0.5 / 256)

    for copy in b2_y:
        net.wait_recv(copy)

    def unpack_b(xd, _):
        for x in range(X2):
            at = X2 * xd + x
            b = region(raw_b, xd, x)
            b2[at] = b
            u2[at + 1, 8 : 8 + ROWS] = st2[7, at] * b
        return 0

    loop(nx, unpack_b)

    def remainder(u_ref, b_ref, st, x, step):
        u, us = region_sides(u_ref, x, step)
        return b_ref[x] - st[6, x] * u + weighted([st[i, x] for i in range(6)], us)

    def down(u_ref, b_ref, st, step, next_b, next_u, next_st):
        def one(x, _):
            r = remainder(u_ref, b_ref, st, 2 * x, step) + remainder(u_ref, b_ref, st, 2 * x + 1, step)
            b = coarse(r, step)
            next_b[x] = b
            next_u[x + 1, 8 : 8 + ROWS] = next_st[7, x] * b
            return 0

        loop(next_b.shape[0], one)

    down(u2, b2, st2, 1, b3, u3, st3)
    down(u3, b3, st3, 2, b4, wa, st4)

    def relaxed(field, b, st, x, step, first=8, rows=ROWS, at=0):
        v, vs = region_sides(field, x, step, first, rows)
        s = weighted([st[i, x, at : at + rows] for i in range(6)], vs)
        return (1.0 - OMEGA) * v + st[7, x, at : at + rows] * (b[x, at : at + rows] + s)

    for src, dst in ((wa, wb), (wb, wa), (wa, wb)):

        def sweep(x, _):
            dst[x + 1, 8 : 8 + ROWS] = relaxed(src, b4, st4, x, 4)
            return 0

        loop(nx, sweep)

    near, span = OWN - 8, 24

    def up3(x, _):
        v3[x + 1, 8 : 8 + ROWS] = u3[x + 1, 8 : 8 + ROWS] + wb[x // 2 + 1, 8 : 8 + ROWS]
        return 0

    loop(2 * nx, up3)

    def relax3(x, _):
        w3[x] = relaxed(v3, b3, st3, x, 2, 8 + near, span, near)
        return 0

    loop(2 * nx, relax3)

    def up2(x, _):
        v2[x + 1, 8 : 8 + span] = u2[x + 1, 8 + near : 8 + near + span] + w3[x // 2]
        return 0

    loop(4 * nx, up2)

    def relax2(x, _):
        w2[x + 1] = relaxed(v2, b2, st2, x, 1, 8, span, near)
        return 0

    loop(4 * nx, relax2)

    wide = lax.dot_general(
        w2[pl.ds(X2 * ix, X2 + 2)].reshape((X2 + 2) * span, LANES), spread[...], (((1,), (0,)), ((), ())),
        precision=lax.Precision.HIGHEST, preferred_element_type=F32,
    ).reshape(X2 + 2, span, 2 * LANES)
    for x in range(X1 + 2):
        m = wide[(x + 1) // 2, :, :LANES]
        rw1[x, pl.ds(8, Y2, stride=2)] = m[8 : 8 + Y2]
        rw1[x, pl.ds(9, Y2, stride=2)] = m[8 : 8 + Y2]
        rw1[x, 7:8] = m[7:8]
        rw1[x, 8 + Y1 : 9 + Y1] = m[8 + Y2 : 9 + Y2]
        v1[x] = u1[x] + rw1[x]
    for x in range(X2):
        h = wide[x + 1, 8 : 8 + Y2, LANES:]
        hw1[x, pl.ds(0, Y2, stride=2)] = h
        hw1[x, pl.ds(1, Y2, stride=2)] = h

    def up1(x, acc):
        halo = unpack_z(both_u, 2 * x, 2, 2) + hw1[x // 2]
        v, vs = sides1(v1, x, halo)
        w = (1.0 - OMEGA) * v + st1[7, x] * (b1[x] + weighted([st1[i, x] for i in range(6)], vs))
        rw0[x, pl.ds(0, Y1, stride=2)] = w
        rw0[x, pl.ds(1, Y1, stride=2)] = w
        for d in range(2):
            v = smooth[2 * x + d + 1, 8 : 8 + Y0] + rw0[x]
            v0[2 * x + d + 1, 8 : 8 + Y0] = v
            acc = pack_z(acc, v, 4 * (2 * x + d), 1)
        return acc

    zs0[2, :8] = loop(X1, up1, zero)

    round_f = faces0(v0, 2)
    round_f.start()
    round_f.wait()
    both_v = merge_z([zr0[2, 0, :8], zr0[2, 1, :8]], 1)

    def last(x, acc):
        v, vs = stencil_sides0(v0, x, both_v)
        s = (1.0 - OMEGA) * v + st0[7, x] * (rhs[x] + weighted([st0[i, x] for i in range(6)], vs))
        sol[x + 1, 8 : 8 + Y0] = s
        return pack_z(acc, s, 4 * x, 1)

    zs0[3, :8] = loop(X0, last, zero)

    round_g = faces0(sol, 3)
    round_g.start()
    out_sol = pltpu.make_async_copy(sol.at[inner0], sol_hbm, local_sems.at[3])
    out_sol.start()
    round_g.wait()
    both_x = merge_z([zr0[3, 0, :8], zr0[3, 1, :8]], 1)

    def residual(x, _):
        res[x] = remainder0(sol, x, both_x)
        return 0

    loop(X0, residual)
    out_res = pltpu.make_async_copy(res, res_hbm, local_sems.at[4])
    out_res.start()
    net.finish()
    out_sol.wait()
    out_res.wait()


def scratch(nx):
    def vmem(*shape):
        return pltpu.VMEM(shape + (LANES,), F32)

    padded0 = (X0 + 2, Y0 + 16)
    padded1 = (X1 + 2, Y1 + 16)
    n2, n3, n4, tall = 4 * nx, 2 * nx, nx, ROWS + 16
    reach = 2 * REACH + 1
    return [
        vmem(X0, Y0), vmem(2, *padded0), vmem(*padded0), vmem(*padded0), vmem(*padded0), vmem(X0, Y0),
        vmem(8, X0, Y0), vmem(4, 16), vmem(4, 2, 16),
        vmem(*padded1), vmem(*padded1), vmem(*padded1), vmem(*padded1), vmem(X1, Y1), vmem(8, X1, Y1),
        vmem(X1, Y0), vmem(X2, Y1), vmem(X1, Y0), vmem(2, 8), vmem(2, 2, 8),
        vmem(X2 * LANES), pltpu.VMEM((LANES, 2 * LANES), F32),
        vmem(reach, nx, 3, 8), vmem(reach, nx, 3, 8),
        vmem(n2 + 2, tall), vmem(n2 + 2, tall), vmem(n2, ROWS), vmem(8, n2, ROWS),
        vmem(n3 + 2, tall), vmem(n3 + 2, tall), vmem(n3 + 2, tall), vmem(n3, ROWS), vmem(8, n3, ROWS),
        vmem(n4 + 2, tall), vmem(n4 + 2, tall), vmem(n4 + 2, tall), vmem(n4, ROWS), vmem(8, n4, ROWS),
        vmem(n3, 24), vmem(n2 + 2, 40), vmem(n2 + 2, 24),
        pltpu.SemaphoreType.DMA((5,)), pltpu.SemaphoreType.DMA((SEMS,)), pltpu.SemaphoreType.DMA((SEMS,)),
    ]


def solution(mesh):
    sizes = tuple(mesh.shape[a] for a in ("gx", "gy", "gz"))
    block = jax.ShapeDtypeStruct((X0, Y0, LANES), F32)
    spec = P("gx", "gy", "gz")

    def shards(right_side, dielectric, guess):
        return pl.pallas_call(
            functools.partial(kernel, sizes),
            out_shape=(block, block),
            in_specs=[pl.BlockSpec(memory_space=pl.ANY)] * 3,
            out_specs=[pl.BlockSpec(memory_space=pl.ANY)] * 2,
            scratch_shapes=scratch(sizes[0]),
            compiler_params=pltpu.CompilerParams(
                collective_id=0, has_side_effects=True, vmem_limit_bytes=40 * 2**20
            ),
            name="vcycle",
        )(right_side, dielectric, guess)

    return jax.shard_map(
        shards, mesh=mesh, in_specs=(spec, spec, spec), out_specs=(spec, spec), check_vma=False
    )
```

time: 506 us -> 44.3 us (0.09)
  starting transfers between devices: 297 us -> 0 us
  waiting for transfers between devices: 122 us -> 0 us
  local copies, waits for them, and re-layouts: 47.3 us -> 4.25 us
  Pallas kernels: 0 us -> 39.2 us
  other arithmetic: 33.6 us -> 0 us
    ppermute x108 -> x0, starting transfers between devices: 297 us -> none  [the longest x54 212 us: extended(): lax.ppermute(tail, axis, [(i, (i + 1) % count) for i in range(ends)])]
    ppermute x108 -> x0, waiting for transfers between devices: 122 us -> none  [the longest x54 102 us: extended(): lax.ppermute(head, axis, [((i + 1) % count, i) for i in range(ends)])]
    reshape x10 -> x0, local copies, waits for them, and re-layouts: 41.3 us -> none  [the longest x4 40.2 us: coarsen(): values.reshape(span_first // 2, 2, span_second // 2, 2, span_third // 2, 2)]
    pallas_call x0 -> x1, Pallas kernels: none -> 39.2 us  [shards(): pl.pallas_call(functools.partial(kernel, sizes), out_shape=(block, block)...]
    reduce_sum x10 -> x0, other arithmetic: 16.3 us -> none  [coarsen(): return jnp.mean(blocks, axis=(1, 3, 5))]
    add x12 -> x0, other arithmetic: 7.05 us -> none  [the longest x7 5.39 us: relax(): values + OMEGA * (source - apply_operator(padder(values), stencil)) / ste...]
  transfers between devices with their start and end apart: 108 -> 0, of which waited for: 41 -> 0; matrix products, arithmetic and copies ran while one was open for 8% -> 0% of each run, Pallas kernels for 0% -> 0%
where the time goes in v1:
time: 44.3 us; the launch traced here: 44.1 us
  Pallas kernels  39.2 us (88%)
  local copies, waits for them, and re-layouts  4.25 us (10%)
  between operations  0.65 us (1%)
    pallas_call x1, Pallas kernels, shards(): pl.pallas_call(functools.partial(kernel, sizes), out_shape=(block, block)...  39.2 us
    unnamed x8, local copies, waits for them, and re-layouts  4.25 us

profile of v1, /device:TPU:1, one launch (start us, length us, event | category | flops | bytes accessed | tf_op | source)
XLA Modules:
  0.0 44.1 jit_solution(10894115550093493534)
XLA Ops:
  0.6 0.0 copy-start
  0.6 0.9 %copy-done = f32[16,32,128]{2,1,0:T(8,128)S(1)} copy-done((f32[16,32,128]{2,1,0:T(8,128)S(1)}, f32[16,32,128]{2,1,0:T(8,128)}, u32[]{:S(2)}) %copy-start) | copy-done | bytes 262168
  1.6 0.0 copy-start.1
  1.6 0.9 %copy-done.1 = f32[16,32,128]{2,1,0:T(8,128)S(1)} copy-done((f32[16,32,128]{2,1,0:T(8,128)S(1)}, f32[16,32,128]{2,1,0:T(8,128)}, u32[]{:S(2)}) %copy-start.1) | copy-done | bytes 262168
  2.5 0.0 copy-start.2
  2.5 0.9 %copy-done.2 = f32[16,32,128]{2,1,0:T(8,128)S(1)} copy-done((f32[16,32,128]{2,1,0:T(8,128)S(1)}, f32[16,32,128]{2,1,0:T(8,128)}, u32[]{:S(2)}) %copy-start.2) | copy-done | bytes 262168
  3.5 39.2 %vcycle.1 = (f32[16,32,128]{2,1,0:T(8,128)S(1)}, f32[16,32,128]{2,1,0:T(8,128)S(1)}) custom-call(f32[16,32,128]{2,1,0:T(8,128)S(1)} %copy-done, f32[16,32,128]{2,1,0:T(8,128)S(1)} %copy-done.1, f32[16,32,128]{2,1,0:T(8,128)S(1)} %copy-done.2), custom_call_target="tpu_custom_call" | custom-call | tf_op jit(solution)/shard_map/vcycle/pallas_call | solution.py:631
  42.7 0.7 %copy.7 = f32[16,32,128]{2,1,0:T(8,128)} copy(f32[16,32,128]{2,1,0:T(8,128)S(1)} %get-tuple-element.4) | data formatting | bytes 524288
  43.4 0.7 %copy.8 = f32[16,32,128]{2,1,0:T(8,128)} copy(f32[16,32,128]{2,1,0:T(8,128)S(1)} %get-tuple-element.5) | data formatting | bytes 524288
Async XLA Ops:
  0.6 1.0 %copy-start = (f32[16,32,128]{2,1,0:T(8,128)S(1)}, f32[16,32,128]{2,1,0:T(8,128)}, u32[]{:S(2)}) copy-start(f32[16,32,128]{2,1,0:T(8,128)} %rhs_hbm.1) | copy-start | bytes 786436
  1.6 0.9 %copy-start.1 = (f32[16,32,128]{2,1,0:T(8,128)S(1)}, f32[16,32,128]{2,1,0:T(8,128)}, u32[]{:S(2)}) copy-start(f32[16,32,128]{2,1,0:T(8,128)} %permit_hbm.1) | copy-start | bytes 786436
  2.5 0.9 %copy-start.2 = (f32[16,32,128]{2,1,0:T(8,128)S(1)}, f32[16,32,128]{2,1,0:T(8,128)}, u32[]{:S(2)}) copy-start(f32[16,32,128]{2,1,0:T(8,128)} %guess_hbm.1) | copy-start | bytes 786436

commit v2 on v1

--- a/solution.py
+++ b/solution.py
@@ -125,7 +125,7 @@
                 made.wait_send()
 
 
-SEMS = 80
+SEMS = 104
 
 
 def pack_z(acc, v, first, w):
@@ -136,6 +136,17 @@
     return acc
 
 
+def cross_z(left, right):
+    odd = iota((8, LANES), 1) % 2 == 1
+    return jnp.where(odd, roll(left, 1, 1), roll(right, LANES - 1, 1))
+
+
+def at_edges(packed, first, tiles):
+    v = jnp.concatenate([roll(packed, LANES - (2 * (first + j) + 1), 1) for j in range(tiles)], axis=0)
+    lane = iota(v.shape, 1)
+    return jnp.where(jnp.logical_or(lane == 0, lane == LANES - 1), v, 0.0)
+
+
 def merge_z(got, w):
     return jnp.where((iota((8, LANES), 1) // w) % 2 == 0, got[0], got[1])
 
@@ -173,7 +184,9 @@
     sizes,
     rhs_hbm, permit_hbm, guess_hbm,
     sol_hbm, res_hbm,
-    rhs, gp, smooth, v0, sol, res, st0, zs0, zr0,
+    rhs, gp, smooth, vn, sol, res, st0, zs0, zr0, part, pack_d, cz,
+    xa, ya, za, xd, yd, zd, xf, yf, zf, exy, exz, eyz, pxy, pxz, pyz,
+    kx, ky, kz, cxz, cyz, rims, crossed,
     p1, u1, v1, rw1, b1, st1, tmp, hw1, rw0, zs1, zr1, pick, spread,
     raw_p, raw_b, p2, u2, b2, st2, p3, u3, v3, b3, st3, p4, wa, wb, b4, st4, w3, v2, w2,
     local_sems, send_sems, recv_sems,
@@ -182,6 +195,7 @@
     net = Net(sizes, send_sems, recv_sems)
     ix, iy, iz = net.me
     inner0 = (pl.ds(1, X0), pl.ds(8, Y0))
+    own0 = slice(8, 8 + Y0)
 
     loads = [
         pltpu.make_async_copy(guess_hbm, gp.at[(0,) + inner0], local_sems.at[0]),
@@ -199,43 +213,122 @@
         def _():
             pl.semaphore_signal(barrier, inc=1, device_id=net.device(way), device_id_type=MESH)
 
-    fields0 = [(gp.at[0], X0, Y0), (gp.at[1], X0, Y0), (smooth, X0, Y0), (v0, X0, Y0), (sol, X0, Y0)]
-    fields1 = [(p1, X1, Y1), (u1, X1, Y1)]
-
-    def clear(fields, zr):
-        for way in ways:
-            out = net.there(way)
-
-            @pl.when(jnp.logical_not(out))
+    signs = (-1, 1)
+    zeros = lambda *shape: jnp.zeros(shape + (LANES,), F32)
+
+    def clear(fields, landings):
+        todo = {}
+        for f, fx, fy in fields:
+            for i, d in enumerate(signs):
+                todo.setdefault((d, 0, 0), []).append((f, (fx + 1 if i else 0,)))
+                todo.setdefault((0, d, 0), []).append((f, (pl.ds(1, fx), pl.ds(8 + fy if i else 7, 1))))
+        for ref, at, way in landings:
+            todo.setdefault(way, []).append((ref, at))
+        for way, items in todo.items():
+
+            @pl.when(jnp.logical_not(net.there(way)))
             def _():
-                side = sum(way) > 0
-                for f, fx, fy in fields:
-                    if way[0]:
-                        f[fx + 1 if side else 0] = jnp.zeros((fy + 16, LANES), F32)
-                    elif way[1]:
-                        at = 8 + fy if side else 7
-                        f[pl.ds(1, fx), pl.ds(at, 1)] = jnp.zeros((fx, 1, LANES), F32)
-                if way[2]:
-                    for r in range(zr.shape[0]):
-                        zr[r, 1 if side else 0] = jnp.zeros(zr.shape[2:], F32)
-
-    clear(fields0, zr0)
-
-    loads[0].wait()
-    loads[1].wait()
-
-    def pack_gp(x, accs):
-        return tuple(pack_z(a, gp[i, x + 1, 8 : 8 + Y0], 4 * x, 1) for i, a in enumerate(accs))
-
-    zero = jnp.zeros((8, LANES), F32)
-    accs = loop(X0, pack_gp, (zero, zero))
-    zs0[0, :8] = accs[0]
-    zs0[0, 8:] = accs[1]
+                for ref, at in items:
+                    ref[at] = jnp.zeros(ref.at[at].shape, F32)
+
+    def landings(x, y, z):
+        return [(ref, (i,), tuple(d if n == axis else 0 for n in range(3)))
+                for axis, ref in enumerate((x, y, z)) for i, d in enumerate(signs)]
+
+    def edge_landings(xy, xz, yz):
+        out = []
+        for i, d in enumerate(signs):
+            for j, e in enumerate(signs):
+                out += [(xy, (i, j), (d, e, 0)), (xz, (i, j), (d, 0, e)), (yz, (i, j), (0, d, e))]
+        return out
+
+    def zero_halo(f, lead=()):
+        for x in (0, X0 + 1):
+            f[lead + (x,)] = zeros(Y0 + 16)
+
+        def one(x, _):
+            f[lead + (x + 1, slice(0, 8))] = zeros(8)
+            f[lead + (x + 1, slice(8 + Y0, 16 + Y0))] = zeros(8)
+            return 0
+
+        loop(X0, one)
+
+    zero_halo(gp, (0,))
+    zero_halo(gp, (1,))
+    clear([], landings(xa, ya, za))
+
+    for load in loads:
+        load.wait()
+
+    lane0 = iota((Y0, LANES), 1)
+
+    def couplings(scale, p, ns):
+        cs = [scale * (p + n) for n in ns]
+        return cs, cs[0] + cs[1] + cs[2] + cs[3] + cs[4] + cs[5]
+
+    def inside0(field, x, lead=()):
+        v = field[lead + (x + 1, pl.ds(8, Y0))]
+        return v, sides(field, x, Y0, 8, 1, roll(v, 1, 1), roll(v, LANES - 1, 1), lead=lead)
+
+    def sum0(x, vs):
+        return weighted([st0[i, x] for i in range(6)], vs)
+
+    def first(x, accs):
+        p, ns = inside0(gp, x, (1,))
+        ns = ns[:4] + (jnp.where(lane0 == 0, 0.0, ns[4]), jnp.where(lane0 == LANES - 1, 0.0, ns[5]))
+        cs, diag = couplings(0.5, p, ns)
+        cs[4] = jnp.where(lane0 == 0, 0.0, cs[4])
+        cs[5] = jnp.where(lane0 == LANES - 1, 0.0, cs[5])
+        for i, c in enumerate(cs):
+            st0[i, x] = c
+        st0[6, x] = diag
+        v, vs = inside0(gp, x, (0,))
+        part[x] = rhs[x] + weighted(cs, vs)
+        return pack_z(accs[0], v, 4 * x, 1), pack_z(accs[1], p, 4 * x, 1)
+
+    zero = zeros(8)
+    accs = loop(X0, first, (zero, zero))
+    zs0[0, 0] = accs[0]
+    zs0[0, 1] = accs[1]
 
     pl.semaphore_wait(barrier, sum(net.there(way).astype(jnp.int32) for way in ways))
 
-    round_a = Faces(net, gp, zs0.at[0], zr0.at[0], X0, Y0)
-    round_a.start()
+    def face_copies(field, lead, x_to, y_to, z_from, z_to):
+        copies = []
+        for i, d in ((1, 1), (0, -1)):
+            copies.append(net.copy(z_from, z_to(1 - i), (0, 0, d)))
+        for i, d in ((1, 1), (0, -1)):
+            copies.append(net.copy(field.at[lead + (X0 if i else 1, pl.ds(8, Y0))], x_to(1 - i), (d, 0, 0)))
+        for i, d in ((1, 1), (0, -1)):
+            row = 7 + Y0 if i else 8
+            copies.append(net.copy(field.at[lead + (pl.ds(1, X0), pl.ds(row, 1))], y_to(1 - i), (0, d, 0)))
+        return copies
+
+    def edge_copies(field, lead, packed, xy, xz, yz):
+        copies = []
+        for i, d in enumerate(signs):
+            for j, e in enumerate(signs):
+                copies.append(net.copy(packed, xz.at[1 - i, 1 - j], (d, 0, e)))
+                copies.append(net.copy(packed, yz.at[1 - i, 1 - j], (0, d, e)))
+        for i, d in enumerate(signs):
+            for j, e in enumerate(signs):
+                line = field.at[lead + (X0 if i else 1, pl.ds(7 + Y0 if j else 8, 1))]
+                copies.append(net.copy(line, xy.at[1 - i, 1 - j, pl.ds(0, 1)], (d, e, 0)))
+        return copies
+
+    def start(copies):
+        for copy in copies:
+            net.start(copy)
+
+    def wait(copies):
+        for copy in copies:
+            net.wait_recv(copy)
+
+    round_a = face_copies(
+        gp, (slice(None),), lambda i: xa.at[i], lambda i: ya.at[i, :, :, pl.ds(0, 1)],
+        zs0.at[0], lambda i: za.at[i],
+    )
+    start(round_a)
 
     def coarse_p1(x, acc):
         tmp[x] = gp[1, 2 * x + 1, 8 : 8 + Y0] + gp[1, 2 * x + 2, 8 : 8 + Y0]
@@ -244,7 +337,9 @@
         p1[x + 1, 8 : 8 + Y1] = v
         return pack_z(acc, v, 2 * x, 2)
 
-    clear(fields1, zr1)
+    clear([(p1, X1, Y1), (u1, X1, Y1), (smooth, X0, Y0)], [
+        (zr, (r, i), (0, 0, d)) for zr, n in ((zr1, 2), (zr0, 1)) for r in range(n) for i, d in enumerate(signs)
+    ])
     zs1[0] = loop(X1, coarse_p1, zero)
     faces_p1 = Faces(net, p1, zs1.at[0], zr1.at[0], X1, Y1)
     faces_p1.start()
@@ -269,61 +364,80 @@
             precision=lax.Precision.HIGHEST, preferred_element_type=F32,
         )
 
+    steps = [d for k in range(1, REACH + 1) for d in (k, -k)]
     for raw in (raw_p, raw_b):
-        for yd in range(2 * REACH + 1):
-            if yd != REACH:
-                d = yd - REACH
-
-                @pl.when(jnp.logical_not(net.there((0, d, 0))))
-                def _():
-                    raw[yd] = jnp.zeros(raw.shape[1:], F32)
-
-        for zd in (0, 2):
-
-            @pl.when(jnp.logical_not(net.there((0, 0, zd - 1))))
+        raw[0, :, :, :4] = zeros(nx, 3, 4)
+        raw[2 * REACH, :, :, 4:] = zeros(nx, 3, 4)
+        for d in steps:
+
+            @pl.when(jnp.logical_not(net.there((0, d, 0))))
+            def _():
+                raw[REACH + d] = zeros(nx, 3, 8)
+
+        for d in signs:
+
+            @pl.when(jnp.logical_not(net.there((0, 0, d))))
             def _():
                 if raw is raw_p:
-                    raw[REACH, ix, zd] = jnp.zeros((8, LANES), F32)
+                    raw[REACH, ix, 1 + d] = zeros(8)
                 else:
-                    raw[REACH, :, zd] = jnp.zeros((nx, 8, LANES), F32)
+                    raw[REACH, :, 1 + d] = zeros(nx, 8)
+
+    def along_y(raw):
+        copies = []
+        for d in steps:
+            src, dst = raw.at[REACH], raw.at[REACH - d]
+            if abs(d) == REACH:
+                rows = pl.ds(4 if d > 0 else 0, 4)
+                src, dst = src.at[:, :, rows], dst.at[:, :, rows]
+            copies.append(net.copy(src, dst, (0, d, 0)))
+        return copies
 
     raw_p[REACH, ix, 1] = compact(lambda x: p1[x + 1, 8 : 8 + Y1])
     p2_z = [net.copy(raw_p.at[REACH, ix, 1], raw_p.at[REACH, ix, 1 - d], (0, 0, d)) for d in (1, -1)]
     for copy in p2_z:
         net.start(copy)
-    loads[2].wait()
-
-    def couplings(scale, p, ns):
-        cs = [scale * (p + n) for n in ns]
-        return cs, cs[0] + cs[1] + cs[2] + cs[3] + cs[4] + cs[5]
-
-    round_a.wait()
-    both_g = merge_z([zr0[0, 0, :8], zr0[0, 1, :8]], 1)
-    both_p = merge_z([zr0[0, 0, 8:], zr0[0, 1, 8:]], 1)
-
-    def stencil_sides0(field, x, both, lead=()):
-        v = field[lead + (x + 1, pl.ds(8, Y0))]
-        return v, sides(field, x, Y0, 8, 1, *z_sides(v, unpack_z(both, 4 * x, 4, 1), 1), lead=lead)
-
-    def first(x, acc):
-        p, ns = stencil_sides0(gp, x, both_p, (1,))
-        cs, diag = couplings(0.5, p, ns)
-        for i, c in enumerate(cs):
-            st0[i, x] = c
+    zero_halo(vn, (0,))
+
+    wait(round_a)
+    own_p = zs0[0, 1]
+    cross_p = cross_z(za[0, 1], za[1, 1])
+    cz[...] = 0.5 * (own_p + cross_p)
+    z_part = cz[...] * cross_z(za[0, 0], za[1, 0])
+    z_diag = 0.5 * cross_p
+    ends = ((0, 0), (1, X0 - 1))
+    rows0 = ((0, 0), (1, Y0 - 1))
+    for i, x in ends:
+        ph = xa[i, 1]
+        c = 0.5 * (gp[1, x + 1, own0] + ph)
+        st0[i, x] = c
+        st0[6, x] += 0.5 * ph
+        part[x] += c * xa[i, 0]
+
+    def first_y(x, _):
+        for i, y in rows0:
+            row = slice(y, y + 1)
+            ph = ya[i, 1, x, :1]
+            c = 0.5 * (gp[1, x + 1, 8 + y : 9 + y] + ph)
+            st0[2 + i, x, row] = c
+            st0[6, x, row] += 0.5 * ph
+            part[x, row] += c * ya[i, 0, x, :1]
+        return 0
+
+    loop(X0, first_y)
+
+    def first_z(x, acc):
+        diag = st0[6, x] + at_edges(z_diag, 4 * x, 4)
         inv = OMEGA / diag
         st0[6, x] = diag
         st0[7, x] = inv
-        v, vs = stencil_sides0(gp, x, both_g, (0,))
-        s = (1.0 - OMEGA) * v + inv * (rhs[x] + weighted(cs, vs))
-        smooth[x + 1, 8 : 8 + Y0] = s
+        s = (1.0 - OMEGA) * gp[0, x + 1, own0] + inv * (part[x] + at_edges(z_part, 4 * x, 4))
+        smooth[x + 1, own0] = s
         return pack_z(acc, s, 4 * x, 1)
 
-    zs0[1, :8] = loop(X0, first, zero)
-
-    def faces0(field, r):
-        return Faces(net, field, zs0.at[r, pl.ds(0, 8)], zr0.at[r, :, pl.ds(0, 8)], X0, Y0)
-
-    round_b = faces0(smooth, 1)
+    zs0[1, 0] = loop(X0, first_z, zero)
+
+    round_b = Faces(net, smooth, zs0.at[1, 0], zr0.at[0], X0, Y0)
     round_b.start()
 
     faces_p1.wait()
@@ -344,15 +458,18 @@
 
     loop(X1, couple1)
 
+    pack_d[...] = loop(X0, lambda x, acc: pack_z(acc, st0[6, x], 4 * x, 1), zero)
+
     round_b.wait()
-    both_s = merge_z([zr0[1, 0, :8], zr0[1, 1, :8]], 1)
-
-    def remainder0(field, x, both):
-        v, vs = stencil_sides0(field, x, both)
-        return rhs[x] - st0[6, x] * v + weighted([st0[i, x] for i in range(6)], vs)
+
+    def remainder0(field, x, z_sum):
+        v, vs = inside0(field, x)
+        return rhs[x] - st0[6, x] * v + sum0(x, vs) + at_edges(z_sum, 4 * x, 4)
+
+    sum_s = cz[...] * cross_z(zr0[0, 0], zr0[0, 1])
 
     def down0(x, acc):
-        tmp[x] = remainder0(smooth, 2 * x, both_s) + remainder0(smooth, 2 * x + 1, both_s)
+        tmp[x] = remainder0(smooth, 2 * x, sum_s) + remainder0(smooth, 2 * x + 1, sum_s)
         b = tmp[x, pl.ds(0, Y1, stride=2)] + tmp[x, pl.ds(1, Y1, stride=2)]
         b = 0.125 * pair_sum(b, 1, 1)
         b1[x] = b
@@ -368,8 +485,17 @@
     for copy in p2_z:
         net.wait_recv(copy)
     p2_x = [net.copy(raw_p.at[REACH, ix], raw_p.at[REACH, ix], (0, 0, 0), k) for k in range(1, nx)]
-    for copy in p2_x:
-        net.start(copy)
+    start(p2_x)
+
+    clear([], landings(xd, yd, zd) + landings(xf, yf, zf) + edge_landings(exy, exz, eyz) + edge_landings(pxy, pxz, pyz))
+    static = edge_copies(gp, (1,), zs0.at[0, 1], pxy, pxz, pyz)
+    for i, d in ((1, 1), (0, -1)):
+        static.append(net.copy(pack_d, zd.at[1 - i], (0, 0, d)))
+        static.append(net.copy(st0.at[6, X0 - 1 if i else 0], xd.at[1 - i], (d, 0, 0)))
+        static.append(net.copy(
+            st0.at[6, :, pl.ds(Y0 - 1 if i else 0, 1)], yd.at[1 - i, :, pl.ds(0, 1)], (0, d, 0)
+        ))
+    start(static)
 
     round_c.wait()
     both_u = merge_z(zr1[1], 2)
@@ -391,16 +517,64 @@
 
     for copy in p2_x:
         net.wait_recv(copy)
-    steps = [d for k in range(1, REACH + 1) for d in (k, -k)]
-    p2_y = [net.copy(raw_p.at[REACH], raw_p.at[REACH - d], (0, d, 0)) for d in steps]
-    for copy in p2_y:
-        net.start(copy)
-
-    for copy in b2_xz:
-        net.wait_recv(copy)
-    b2_y = [net.copy(raw_b.at[REACH], raw_b.at[REACH - d], (0, d, 0)) for d in steps]
-    for copy in b2_y:
-        net.start(copy)
+    p2_y = along_y(raw_p)
+    start(p2_y)
+
+    wait(static)
+    lane8, row8 = iota((8, LANES), 1), iota((8, LANES), 0)
+
+    def inverse(p, diag):
+        inside = p > 0.0
+        return jnp.where(inside, OMEGA / jnp.where(inside, diag, 1.0), 0.0)
+
+    def to_z_faces(x_edges, y_edges):
+        return (
+            roll(x_edges[0], 8, 1), roll(x_edges[1], LANES - 8, 1),
+            roll(roll(y_edges[0], LANES - 6, 1), 1, 0), roll(roll(y_edges[1], 6, 1), 7, 0),
+        )
+
+    quarter = (lane8 // 2) % 4
+    z_masks = (
+        lane8 < 8, lane8 >= LANES - 8,
+        jnp.logical_and(quarter == 0, row8 == 0), jnp.logical_and(quarter == 3, row8 == 7),
+    )
+    far_x = ((0, X0 - 1), (1, 0))
+    far_y = ((0, 3, 7), (1, 0, 0))
+    kz[...] = inverse(cross_p, cross_z(zd[0], zd[1]))
+    edge_x = [cross_z(pxz[i, 0], pxz[i, 1]) for i in range(2)]
+    edge_y = [cross_z(pyz[i, 0], pyz[i, 1]) for i in range(2)]
+    for n, (mask, p) in enumerate(zip(z_masks, to_z_faces(edge_x, edge_y))):
+        rims[n] = jnp.where(mask, 0.5 * (cross_p + p), 0.0)
+    edge_lane = jnp.logical_or(lane0 == 0, lane0 == LANES - 1)
+    for i, x in far_x:
+        ph = xa[i, 1]
+        kx[i] = inverse(ph, xd[i])
+        cxz[i] = jnp.where(edge_lane, 0.5 * (ph + at_edges(edge_x[i], 4 * x, 4)), 0.0)
+        for j, y in rows0:
+            rims[4 + 2 * i + j, :1] = 0.5 * (ph[y : y + 1] + pxy[i, j, :1])
+    for i, j, r in far_y:
+        crossed[i] = edge_y[i]
+        for k, x in ends:
+            rims[8 + 2 * i + k, :1] = 0.5 * (ya[i, 1, x, :1] + pxy[k, i, :1])
+
+    edge_row = jnp.logical_or(iota((1, LANES), 1) == 0, iota((1, LANES), 1) == LANES - 1)
+
+    def edge_of_y(packed, x, j):
+        return roll(packed, LANES - (2 * (4 * x + j) + 1), 1)
+
+    def static_y(x, _):
+        for i, j, r in far_y:
+            ph = ya[i, 1, x, :1]
+            ky[i, x, :1] = inverse(ph, yd[i, x, :1])
+            p = edge_of_y(crossed[i, r : r + 1], x, j)
+            cyz[i, x, :1] = jnp.where(edge_row, 0.5 * (ph + p), 0.0)
+        return 0
+
+    loop(X0, static_y)
+
+    wait(b2_xz)
+    b2_y = along_y(raw_b)
+    start(b2_y)
 
     for f in (p2, u2, p3, u3, v3, p4, wa, wb):
         n = f.shape[0]
@@ -560,35 +734,82 @@
         rw0[x, pl.ds(0, Y1, stride=2)] = w
         rw0[x, pl.ds(1, Y1, stride=2)] = w
         for d in range(2):
-            v = smooth[2 * x + d + 1, 8 : 8 + Y0] + rw0[x]
-            v0[2 * x + d + 1, 8 : 8 + Y0] = v
+            v = smooth[2 * x + d + 1, own0] + rw0[x]
+            vn[0, 2 * x + d + 1, own0] = v
             acc = pack_z(acc, v, 4 * (2 * x + d), 1)
         return acc
 
-    zs0[2, :8] = loop(X1, up1, zero)
-
-    round_f = faces0(v0, 2)
-    round_f.start()
-    round_f.wait()
-    both_v = merge_z([zr0[2, 0, :8], zr0[2, 1, :8]], 1)
-
-    def last(x, acc):
-        v, vs = stencil_sides0(v0, x, both_v)
-        s = (1.0 - OMEGA) * v + st0[7, x] * (rhs[x] + weighted([st0[i, x] for i in range(6)], vs))
-        sol[x + 1, 8 : 8 + Y0] = s
-        return pack_z(acc, s, 4 * x, 1)
-
-    zs0[3, :8] = loop(X0, last, zero)
-
-    round_g = faces0(sol, 3)
-    round_g.start()
+    zs0[2, 0] = loop(X1, up1, zero)
+
+    round_f = edge_copies(vn, (0,), zs0.at[2, 0], exy, exz, eyz)
+    round_f += face_copies(
+        vn, (0,), lambda i: xf.at[i, 0], lambda i: yf.at[i, 0, :, pl.ds(0, 1)],
+        zs0.at[2, 0], lambda i: zf.at[i, 0],
+    )
+    start(round_f)
+
+    def last_part(x, acc):
+        _, vs = inside0(vn, x, (0,))
+        n = rhs[x] + sum0(x, vs)
+        vn[1, x + 1, own0] = n
+        part[x] = n
+        return pack_z(acc, n, 4 * x, 1)
+
+    zs0[2, 1] = loop(X0, last_part, zero)
+    round_n = face_copies(
+        vn, (1,), lambda i: xf.at[i, 1], lambda i: yf.at[i, 1, :, pl.ds(0, 1)],
+        zs0.at[2, 1], lambda i: zf.at[i, 1],
+    )
+    start(round_n)
+    wait(round_f)
+    wait(round_n)
+
+    edge_x = [cross_z(exz[i, 0], exz[i, 1]) for i in range(2)]
+    edge_y = [cross_z(eyz[i, 0], eyz[i, 1]) for i in range(2)]
+    cross_v = cross_z(zf[0, 0], zf[1, 0])
+    n = cross_z(zf[0, 1], zf[1, 1]) + cz[...] * zs0[2, 0]
+    for k, v in enumerate(to_z_faces(edge_x, edge_y)):
+        n = n + rims[k] * v
+    sum_x = cz[...] * ((1.0 - OMEGA) * cross_v + kz[...] * n)
+    z_part = cz[...] * cross_v
+    row0 = iota((Y0, LANES), 0)
+    for (i, x), (_, far) in zip(ends, far_x):
+        vh = xf[i, 0]
+        n = xf[i, 1] + st0[i, x] * vn[0, x + 1, own0] + cxz[i] * at_edges(edge_x[i], 4 * far, 4)
+        for j, y in rows0:
+            n = n + jnp.where(row0 == y, rims[4 + 2 * i + j, :1] * exy[i, j, :1], 0.0)
+        sol[X0 + 1 if i else 0, own0] = (1.0 - OMEGA) * vh + kx[i] * n
+        part[x] += st0[i, x] * vh
+    for i, j, r in far_y:
+        crossed[i] = edge_y[i]
+        for k, x in ends:
+            yf[i, 1, x, :1] += rims[8 + 2 * i + k, :1] * exy[k, i, :1]
+
+    def last_y(x, _):
+        for (i, y), (_, j, r) in zip(rows0, far_y):
+            row = slice(y, y + 1)
+            vh = yf[i, 0, x, :1]
+            c = st0[2 + i, x, row]
+            n = yf[i, 1, x, :1] + c * vn[0, x + 1, 8 + y : 9 + y]
+            n = n + cyz[i, x, :1] * edge_of_y(crossed[i, r : r + 1], x, j)
+            at = 8 + Y0 if i else 7
+            sol[x + 1, at : at + 1] = (1.0 - OMEGA) * vh + ky[i, x, :1] * n
+            part[x, row] += c * vh
+        return 0
+
+    loop(X0, last_y)
+
+    def last_z(x, _):
+        n = part[x] + at_edges(z_part, 4 * x, 4)
+        sol[x + 1, own0] = (1.0 - OMEGA) * vn[0, x + 1, own0] + st0[7, x] * n
+        return 0
+
+    loop(X0, last_z)
     out_sol = pltpu.make_async_copy(sol.at[inner0], sol_hbm, local_sems.at[3])
     out_sol.start()
-    round_g.wait()
-    both_x = merge_z([zr0[3, 0, :8], zr0[3, 1, :8]], 1)
 
     def residual(x, _):
-        res[x] = remainder0(sol, x, both_x)
+        res[x] = remainder0(sol, x, sum_x)
         return 0
 
     loop(X0, residual)
@@ -608,8 +829,12 @@
     n2, n3, n4, tall = 4 * nx, 2 * nx, nx, ROWS + 16
     reach = 2 * REACH + 1
     return [
-        vmem(X0, Y0), vmem(2, *padded0), vmem(*padded0), vmem(*padded0), vmem(*padded0), vmem(X0, Y0),
-        vmem(8, X0, Y0), vmem(4, 16), vmem(4, 2, 16),
+        vmem(X0, Y0), vmem(2, *padded0), vmem(*padded0), vmem(2, *padded0), vmem(*padded0), vmem(X0, Y0),
+        vmem(8, X0, Y0), vmem(3, 2, 8), vmem(1, 2, 8), vmem(X0, Y0), vmem(8), vmem(8),
+        vmem(2, 2, Y0), vmem(2, 2, X0, 8), vmem(2, 2, 8), vmem(2, Y0), vmem(2, X0, 8), vmem(2, 8),
+        vmem(2, 2, Y0), vmem(2, 2, X0, 8), vmem(2, 2, 8),
+        vmem(2, 2, 8), vmem(2, 2, 8), vmem(2, 2, 8), vmem(2, 2, 8), vmem(2, 2, 8), vmem(2, 2, 8),
+        vmem(2, Y0), vmem(2, X0, 8), vmem(8), vmem(2, Y0), vmem(2, X0, 8), vmem(12, 8), vmem(2, 8),
         vmem(*padded1), vmem(*padded1), vmem(*padded1), vmem(*padded1), vmem(X1, Y1), vmem(8, X1, Y1),
         vmem(X1, Y0), vmem(X2, Y1), vmem(X1, Y0), vmem(2, 8), vmem(2, 2, 8),
         vmem(X2 * LANES), pltpu.VMEM((LANES, 2 * LANES), F32),
@@ -635,7 +860,7 @@
             out_specs=[pl.BlockSpec(memory_space=pl.ANY)] * 2,
             scratch_shapes=scratch(sizes[0]),
             compiler_params=pltpu.CompilerParams(
-                collective_id=0, has_side_effects=True, vmem_limit_bytes=40 * 2**20
+                collective_id=0, has_side_effects=True, vmem_limit_bytes=60 * 2**20
             ),
             name="vcycle",
         )(right_side, dielectric, guess)

time: 44.3 us -> 38.8 us (0.88)
  Pallas kernels: 39.2 us -> 35.6 us
  local copies, waits for them, and re-layouts: 4.25 us -> 2.42 us
    pallas_call x1, Pallas kernels: 39.2 us -> 35.6 us  [shards(): pl.pallas_call(functools.partial(kernel, sizes), out_shape=(block, block)...]
    unnamed x8 -> x4, local copies, waits for them, and re-layouts: 4.25 us -> 2.42 us
where the time goes in v2:
time: 38.8 us; the launch traced here: 38.7 us
  Pallas kernels  35.6 us (92%)
  local copies, waits for them, and re-layouts  2.42 us (6%)
  between operations  0.65 us (2%)
    pallas_call x1, Pallas kernels, shards(): pl.pallas_call(functools.partial(kernel, sizes), out_shape=(block, block)...  35.6 us
    unnamed x4, local copies, waits for them, and re-layouts  2.42 us

profile of v2, /device:TPU:1, one launch (start us, length us, event | category | flops | bytes accessed | tf_op | source)
XLA Modules:
  0.0 38.7 jit_solution(4860585453627610284)
XLA Ops:
  0.6 35.6 %vcycle.1 = (f32[16,32,128]{2,1,0:T(8,128)}, f32[16,32,128]{2,1,0:T(8,128)}) custom-call(f32[16,32,128]{2,1,0:T(8,128)} %rhs_hbm.1, f32[16,32,128]{2,1,0:T(8,128)} %permit_hbm.1, f32[16,32,128]{2,1,0:T(8,128)} %guess_hbm.1), custom_call_target="tpu_custom_call" | custom-call | tf_op jit(solution)/shard_map/vcycle/pallas_call | solution.py:856
  36.2 0.0 copy-start
  36.2 1.7 %copy.7 = f32[16,32,128]{2,1,0:T(8,128)} copy(f32[16,32,128]{2,1,0:T(8,128)} %get-tuple-element.4) | data formatting | bytes 524288
  38.0 0.0 copy-done
  38.0 0.7 %copy.8 = f32[16,32,128]{2,1,0:T(8,128)} copy(f32[16,32,128]{2,1,0:T(8,128)S(1)} %copy-done) | data formatting | bytes 524288
Async XLA Ops:
  36.2 1.7 %copy-start = (f32[16,32,128]{2,1,0:T(8,128)S(1)}, f32[16,32,128]{2,1,0:T(8,128)}, u32[]{:S(2)}) copy-start(f32[16,32,128]{2,1,0:T(8,128)} %get-tuple-element.5) | copy-start | bytes 786436

commit v3 on v2

--- a/solution.py
+++ b/solution.py
@@ -37,19 +37,19 @@
 
 
 class Faces:
-    def __init__(self, net, field, sent, got, nx, ny):
+    def __init__(self, net, field, into, sent, got, nx, ny):
         self.net = net
         self.copies = {}
         lead = (slice(None),) * (len(field.shape) - 3)
         for d in (-1, 1):
             src, dst = (1, nx + 1) if d < 0 else (nx, 0)
             self.copies[(d, 0, 0)] = net.copy(
-                field.at[lead + (src, pl.ds(8, ny))], field.at[lead + (dst, pl.ds(8, ny))], (d, 0, 0)
+                field.at[lead + (src, pl.ds(8, ny))], into.at[lead + (dst, pl.ds(8, ny))], (d, 0, 0)
             )
             src, dst = (8, 8 + ny) if d < 0 else (7 + ny, 7)
             self.copies[(0, d, 0)] = net.copy(
                 field.at[lead + (pl.ds(1, nx), pl.ds(src, 1))],
-                field.at[lead + (pl.ds(1, nx), pl.ds(dst, 1))],
+                into.at[lead + (pl.ds(1, nx), pl.ds(dst, 1))],
                 (0, d, 0),
             )
             self.copies[(0, 0, d)] = net.copy(sent, got.at[0 if d > 0 else 1], (0, 0, d))
@@ -187,8 +187,8 @@
     rhs, gp, smooth, vn, sol, res, st0, zs0, zr0, part, pack_d, cz,
     xa, ya, za, xd, yd, zd, xf, yf, zf, exy, exz, eyz, pxy, pxz, pyz,
     kx, ky, kz, cxz, cyz, rims, crossed,
-    p1, u1, v1, rw1, b1, st1, tmp, hw1, rw0, zs1, zr1, pick, spread,
-    raw_p, raw_b, p2, u2, b2, st2, p3, u3, v3, b3, st3, p4, wa, wb, b4, st4, w3, v2, w2,
+    p1, u1, u1h, v1, rw1, b1, st1, tmp, hw1, rw0, zs1, zr1, pick, spread, lhs, select,
+    raw_p, raw_b, raw_e, p2, u2, b2, st2, p3, u3, v3, b3, st3, p4, wa, wb, b4, st4, w3, v2, w2,
     local_sems, send_sems, recv_sems,
 ):
     nx = sizes[0]
@@ -206,8 +206,9 @@
         load.start()
 
     ways = [(0, 0, 1), (0, 0, -1), (1, 0, 0), (-1, 0, 0), (0, 1, 0), (0, -1, 0)]
+    greeted = ways + [(2, 0, 0), (-2, 0, 0)]
     barrier = pltpu.get_barrier_semaphore()
-    for way in ways:
+    for way in greeted:
 
         @net.when(way)
         def _():
@@ -242,16 +243,16 @@
                 out += [(xy, (i, j), (d, e, 0)), (xz, (i, j), (d, 0, e)), (yz, (i, j), (0, d, e))]
         return out
 
-    def zero_halo(f, lead=()):
-        for x in (0, X0 + 1):
-            f[lead + (x,)] = zeros(Y0 + 16)
+    def zero_halo(f, lead=(), fx=X0, fy=Y0):
+        for x in (0, fx + 1):
+            f[lead + (x,)] = zeros(fy + 16)
 
         def one(x, _):
             f[lead + (x + 1, slice(0, 8))] = zeros(8)
-            f[lead + (x + 1, slice(8 + Y0, 16 + Y0))] = zeros(8)
+            f[lead + (x + 1, slice(8 + fy, 16 + fy))] = zeros(8)
             return 0
 
-        loop(X0, one)
+        loop(fx, one)
 
     zero_halo(gp, (0,))
     zero_halo(gp, (1,))
@@ -291,7 +292,7 @@
     zs0[0, 0] = accs[0]
     zs0[0, 1] = accs[1]
 
-    pl.semaphore_wait(barrier, sum(net.there(way).astype(jnp.int32) for way in ways))
+    pl.semaphore_wait(barrier, sum(net.there(way).astype(jnp.int32) for way in greeted))
 
     def face_copies(field, lead, x_to, y_to, z_from, z_to):
         copies = []
@@ -337,11 +338,11 @@
         p1[x + 1, 8 : 8 + Y1] = v
         return pack_z(acc, v, 2 * x, 2)
 
-    clear([(p1, X1, Y1), (u1, X1, Y1), (smooth, X0, Y0)], [
+    clear([(p1, X1, Y1), (u1h, X1, Y1), (smooth, X0, Y0)], [
         (zr, (r, i), (0, 0, d)) for zr, n in ((zr1, 2), (zr0, 1)) for r in range(n) for i, d in enumerate(signs)
     ])
     zs1[0] = loop(X1, coarse_p1, zero)
-    faces_p1 = Faces(net, p1, zs1.at[0], zr1.at[0], X1, Y1)
+    faces_p1 = Faces(net, p1, p1, zs1.at[0], zr1.at[0], X1, Y1)
     faces_p1.start()
 
     for x in range(X2):
@@ -354,43 +355,55 @@
     right = jnp.logical_and(row == 2 * Z2, col < 2)
     spread[:, LANES:] = jnp.logical_or(left, right).astype(F32)
 
+    row, col = iota((LANES, LANES), 0), iota((LANES, LANES), 1)
+    group, place = col // Z2, col % Z2
+    for n, chosen in enumerate((
+        jnp.logical_and(group == 0, row == col + Z2),
+        jnp.logical_and(group == 3, row == col - 3 * Z2),
+        jnp.logical_and(place == 0, row == 3 * Z2 + X2 + group),
+        jnp.logical_and(place == Z2 - 1, row == 3 * Z2 + group),
+    )):
+        select[:, n * LANES : (n + 1) * LANES] = chosen.astype(F32)
+
+    def to_compact(parts):
+        return lax.dot_general(
+            parts, pick[...], (((1,), (0,)), ((), ())),
+            precision=lax.Precision.HIGHEST, preferred_element_type=F32,
+        )
+
     def compact(planes):
         parts = []
         for x in range(X2):
             tmp[x, :Y1] = planes(2 * x) + planes(2 * x + 1)
             parts.append(tmp[x, pl.ds(0, Y2, stride=2)] + tmp[x, pl.ds(1, Y2, stride=2)])
-        return lax.dot_general(
-            jnp.concatenate(parts, axis=1), pick[...], (((1,), (0,)), ((), ())),
-            precision=lax.Precision.HIGHEST, preferred_element_type=F32,
-        )
+        return to_compact(jnp.concatenate(parts, axis=1))
 
     steps = [d for k in range(1, REACH + 1) for d in (k, -k)]
-    for raw in (raw_p, raw_b):
-        raw[0, :, :, :4] = zeros(nx, 3, 4)
-        raw[2 * REACH, :, :, 4:] = zeros(nx, 3, 4)
-        for d in steps:
-
-            @pl.when(jnp.logical_not(net.there((0, d, 0))))
-            def _():
-                raw[REACH + d] = zeros(nx, 3, 8)
-
-        for d in signs:
-
-            @pl.when(jnp.logical_not(net.there((0, 0, d))))
-            def _():
-                if raw is raw_p:
-                    raw[REACH, ix, 1 + d] = zeros(8)
-                else:
-                    raw[REACH, :, 1 + d] = zeros(nx, 8)
-
-    def along_y(raw):
+    raw_p[0, :, :, :4] = zeros(nx, 3, 4)
+    raw_p[2 * REACH, :, :, 4:] = zeros(nx, 3, 4)
+    raw_e[0, :, :, :12] = zeros(nx, 3, 12)
+    raw_e[2 * REACH, :, :, 12:] = zeros(nx, 3, 12)
+    for d in steps:
+
+        @pl.when(jnp.logical_not(net.there((0, d, 0))))
+        def _():
+            raw_p[REACH + d] = zeros(nx, 3, 8)
+            raw_e[REACH + d] = zeros(nx, 3, 24)
+
+    for d in signs:
+
+        @pl.when(jnp.logical_not(net.there((0, 0, d))))
+        def _():
+            raw_p[REACH, ix, 1 + d] = zeros(8)
+            raw_b[:, 1 + d] = zeros(nx, 24)
+
+    def along_y(raw, first, rows, half):
         copies = []
         for d in steps:
-            src, dst = raw.at[REACH], raw.at[REACH - d]
+            span = pl.ds(first, rows)
             if abs(d) == REACH:
-                rows = pl.ds(4 if d > 0 else 0, 4)
-                src, dst = src.at[:, :, rows], dst.at[:, :, rows]
-            copies.append(net.copy(src, dst, (0, d, 0)))
+                span = pl.ds(first + rows - half if d > 0 else first, half)
+            copies.append(net.copy(raw.at[REACH, :, :, span], raw.at[REACH - d, :, :, span], (0, d, 0)))
         return copies
 
     raw_p[REACH, ix, 1] = compact(lambda x: p1[x + 1, 8 : 8 + Y1])
@@ -398,6 +411,8 @@
     for copy in p2_z:
         net.start(copy)
     zero_halo(vn, (0,))
+    zero_halo(u1, (), X1, Y1)
+    lhs[...] = jnp.zeros(lhs.shape, F32)
 
     wait(round_a)
     own_p = zs0[0, 1]
@@ -437,7 +452,7 @@
 
     zs0[1, 0] = loop(X0, first_z, zero)
 
-    round_b = Faces(net, smooth, zs0.at[1, 0], zr0.at[0], X0, Y0)
+    round_b = Faces(net, smooth, smooth, zs0.at[1, 0], zr0.at[0], X0, Y0)
     round_b.start()
 
     faces_p1.wait()
@@ -459,28 +474,6 @@
     loop(X1, couple1)
 
     pack_d[...] = loop(X0, lambda x, acc: pack_z(acc, st0[6, x], 4 * x, 1), zero)
-
-    round_b.wait()
-
-    def remainder0(field, x, z_sum):
-        v, vs = inside0(field, x)
-        return rhs[x] - st0[6, x] * v + sum0(x, vs) + at_edges(z_sum, 4 * x, 4)
-
-    sum_s = cz[...] * cross_z(zr0[0, 0], zr0[0, 1])
-
-    def down0(x, acc):
-        tmp[x] = remainder0(smooth, 2 * x, sum_s) + remainder0(smooth, 2 * x + 1, sum_s)
-        b = tmp[x, pl.ds(0, Y1, stride=2)] + tmp[x, pl.ds(1, Y1, stride=2)]
-        b = 0.125 * pair_sum(b, 1, 1)
-        b1[x] = b
-        u = st1[7, x] * b
-        u1[x + 1, 8 : 8 + Y1] = u
-        return pack_z(acc, u, 2 * x, 2)
-
-    zs1[1] = loop(X1, down0, zero)
-
-    round_c = Faces(net, u1, zs1.at[1], zr1.at[1], X1, Y1)
-    round_c.start()
 
     for copy in p2_z:
         net.wait_recv(copy)
@@ -497,31 +490,77 @@
         ))
     start(static)
 
-    round_c.wait()
-    both_u = merge_z(zr1[1], 2)
+    round_b.wait()
+
+    def remainder0(field, x, z_sum):
+        v, vs = inside0(field, x)
+        return rhs[x] - st0[6, x] * v + sum0(x, vs) + at_edges(z_sum, 4 * x, 4)
+
+    sum_s = cz[...] * cross_z(zr0[0, 0], zr0[0, 1])
+
+    def down0(x, acc):
+        tmp[x] = remainder0(smooth, 2 * x, sum_s) + remainder0(smooth, 2 * x + 1, sum_s)
+        b = tmp[x, pl.ds(0, Y1, stride=2)] + tmp[x, pl.ds(1, Y1, stride=2)]
+        b = 0.125 * pair_sum(b, 1, 1)
+        b1[x] = b
+        u = st1[7, x] * b
+        u1[x + 1, 8 : 8 + Y1] = u
+        return pack_z(acc, u, 2 * x, 2)
+
+    zs1[1] = loop(X1, down0, zero)
+
+
+    lane16 = iota((Y1, LANES), 1)
+    nothing = jnp.zeros((Y1, LANES), F32)
 
     def remainder1(x):
-        u, us = sides1(u1, x, unpack_z(both_u, 2 * x, 2, 2))
+        u, us = sides1(u1, x, nothing)
         return b1[x] - st1[6, x] * u + weighted([st1[i, x] for i in range(6)], us)
 
-    raw_b[REACH, ix, 1] = compact(remainder1)
-
-    mine = raw_b.at[REACH, ix, 1]
+    def halves(v, at):
+        tmp[at, :Y1] = v
+        return tmp[at, pl.ds(0, Y2, stride=2)] + tmp[at, pl.ds(1, Y2, stride=2)]
+
+    lane8 = iota((8, LANES), 1)
+    z_out = zero
+    for x in range(X2):
+        cols = pl.ds(x * LANES, LANES)
+        lhs[:8, cols] = halves(remainder1(2 * x) + remainder1(2 * x + 1), x)
+        for i, y in ((0, 0), (1, Y1 - 1)):
+            lhs[8 + i : 9 + i, cols] = sum(
+                st1[2 + i, k, y : y + 1] * u1[k + 1, 8 + y : 9 + y] for k in (2 * x, 2 * x + 1)
+            )
+        out = [
+            jnp.where(lane16 == 0, st1[4, k], jnp.where(lane16 == LANES - 1, st1[5, k], 0.0)) * u1[k + 1, 8 : 8 + Y1]
+            for k in (2 * x, 2 * x + 1)
+        ]
+        out = 0.125 * halves(out[0] + out[1], X2 + x)
+        z_out = z_out + jnp.where(lane8 == 3 * Z2 + x, roll(out, 3 * Z2 + x, 1), 0.0)
+        z_out = z_out + jnp.where(lane8 == 3 * Z2 + X2 + x, roll(out, 3 * Z2 + X2 + 1 + x, 1), 0.0)
+    for i, x in ((0, 0), (1, X1 - 1)):
+        lhs[16:, i * LANES : (i + 1) * LANES] = halves(st1[i, x] * u1[x + 1, 8 : 8 + Y1], i)
+    known = to_compact(lhs[...])
+    raw_b[ix, 1, :16] = known[:16]
+    raw_b[ix, 1, 16:] = known[16:] + z_out
+
+    mine = raw_b.at[ix, 1]
     b2_xz = []
     for d in (1, -1, 0):
         for k in range(nx):
             if d or k:
-                b2_xz.append(net.copy(mine, raw_b.at[REACH, ix, 1 - d], (0, 0, d), k))
-    for copy in b2_xz:
-        net.start(copy)
+                b2_xz.append(net.copy(mine, raw_b.at[ix, 1 - d], (0, 0, d), k))
+    start(b2_xz)
+
+    round_c = Faces(net, u1, u1h, zs1.at[1], zr1.at[1], X1, Y1)
+    round_c.start()
 
     for copy in p2_x:
         net.wait_recv(copy)
-    p2_y = along_y(raw_p)
+    p2_y = along_y(raw_p, 0, 8, 4)
     start(p2_y)
 
     wait(static)
-    lane8, row8 = iota((8, LANES), 1), iota((8, LANES), 0)
+    row8 = iota((8, LANES), 0)
 
     def inverse(p, diag):
         inside = p > 0.0
@@ -573,7 +612,26 @@
     loop(X0, static_y)
 
     wait(b2_xz)
-    b2_y = along_y(raw_b)
+    crossing = lax.dot_general(
+        raw_b[:, :, 16:].reshape(nx * 24, LANES), select[...], (((1,), (0,)), ((), ())),
+        precision=lax.Precision.HIGHEST, preferred_element_type=F32,
+    ).reshape(nx, 3, 8, 4 * LANES)
+    across = lambda n, xd, zd: crossing[xd, zd, :, n * LANES : (n + 1) * LANES]
+    for xd in range(nx):
+        for zd in range(3):
+            b = raw_b[xd, zd, :8]
+            if xd > 0:
+                b = b + across(0, xd - 1, zd)
+            if xd < nx - 1:
+                b = b + across(1, xd + 1, zd)
+            if zd > 0:
+                b = b + across(2, xd, zd - 1)
+            if zd < 2:
+                b = b + across(3, xd, zd + 1)
+            raw_e[REACH, xd, zd, 8:16] = b
+            raw_e[REACH, xd, zd, 7:8] = raw_b[xd, zd, 8:9]
+            raw_e[REACH, xd, zd, 16:17] = raw_b[xd, zd, 9:10]
+    b2_y = along_y(raw_e, 7, 10, 5)
     start(b2_y)
 
     for f in (p2, u2, p3, u3, v3, p4, wa, wb):
@@ -590,19 +648,18 @@
     for f in (v2, w2):
         loop(f.shape[0], lambda x, _: f.__setitem__(x, jnp.zeros(f.shape[1:], F32)) or 0)
 
-    def region(raw, xd, x):
+    def region(blocks, x):
         lane = iota((ROWS, LANES), 1)
-        part = [
-            roll(raw[:, xd, zd].reshape(ROWS, LANES), Z2 * (zd - x), 1) for zd in range(3)
-        ]
+        part = [roll(blocks[zd], Z2 * (zd - x), 1) for zd in range(3)]
         return jnp.where(lane < Z2, part[0], jnp.where(lane < 2 * Z2, part[1], jnp.where(lane < 3 * Z2, part[2], 0.0)))
 
     for copy in p2_y:
         net.wait_recv(copy)
 
     def unpack_p(xd, _):
+        blocks = [raw_p[:, xd, zd].reshape(ROWS, LANES) for zd in range(3)]
         for x in range(X2):
-            p2[X2 * xd + x + 1, 8 : 8 + ROWS] = region(raw_p, xd, x)
+            p2[X2 * xd + x + 1, 8 : 8 + ROWS] = region(blocks, x)
         return 0
 
     loop(nx, unpack_p)
@@ -646,9 +703,20 @@
         net.wait_recv(copy)
 
     def unpack_b(xd, _):
+        blocks = []
+        for zd in range(3):
+            tiles = []
+            for yd in range(2 * REACH + 1):
+                b = raw_e[yd, xd, zd, 8:16]
+                if yd > 0:
+                    b = b + jnp.where(row8 == 0, raw_e[yd - 1, xd, zd, 16:17], 0.0)
+                if yd < 2 * REACH:
+                    b = b + jnp.where(row8 == 7, raw_e[yd + 1, xd, zd, 7:8], 0.0)
+                tiles.append(b)
+            blocks.append(jnp.concatenate(tiles, axis=0))
         for x in range(X2):
             at = X2 * xd + x
-            b = region(raw_b, xd, x)
+            b = region(blocks, x)
             b2[at] = b
             u2[at + 1, 8 : 8 + ROWS] = st2[7, at] * b
         return 0
@@ -721,7 +789,15 @@
         rw1[x, pl.ds(9, Y2, stride=2)] = m[8 : 8 + Y2]
         rw1[x, 7:8] = m[7:8]
         rw1[x, 8 + Y1 : 9 + Y1] = m[8 + Y2 : 9 + Y2]
-        v1[x] = u1[x] + rw1[x]
+    round_c.wait()
+    both_u = merge_z(zr1[1], 2)
+    inner1 = slice(8, 8 + Y1)
+    for x in range(X1):
+        v1[x + 1, inner1] = u1[x + 1, inner1] + rw1[x + 1, inner1]
+        for y in (7, 8 + Y1):
+            v1[x + 1, y : y + 1] = u1h[x + 1, y : y + 1] + rw1[x + 1, y : y + 1]
+    for x in (0, X1 + 1):
+        v1[x, inner1] = u1h[x, inner1] + rw1[x, inner1]
     for x in range(X2):
         h = wide[x + 1, 8 : 8 + Y2, LANES:]
         hw1[x, pl.ds(0, Y2, stride=2)] = h
@@ -835,10 +911,11 @@
         vmem(2, 2, Y0), vmem(2, 2, X0, 8), vmem(2, 2, 8),
         vmem(2, 2, 8), vmem(2, 2, 8), vmem(2, 2, 8), vmem(2, 2, 8), vmem(2, 2, 8), vmem(2, 2, 8),
         vmem(2, Y0), vmem(2, X0, 8), vmem(8), vmem(2, Y0), vmem(2, X0, 8), vmem(12, 8), vmem(2, 8),
-        vmem(*padded1), vmem(*padded1), vmem(*padded1), vmem(*padded1), vmem(X1, Y1), vmem(8, X1, Y1),
+        vmem(*padded1), vmem(*padded1), vmem(*padded1), vmem(*padded1), vmem(*padded1), vmem(X1, Y1), vmem(8, X1, Y1),
         vmem(X1, Y0), vmem(X2, Y1), vmem(X1, Y0), vmem(2, 8), vmem(2, 2, 8),
         vmem(X2 * LANES), pltpu.VMEM((LANES, 2 * LANES), F32),
-        vmem(reach, nx, 3, 8), vmem(reach, nx, 3, 8),
+        pltpu.VMEM((24, X2 * LANES), F32), pltpu.VMEM((LANES, 4 * LANES), F32),
+        vmem(reach, nx, 3, 8), vmem(nx, 3, 24), vmem(reach, nx, 3, 24),
         vmem(n2 + 2, tall), vmem(n2 + 2, tall), vmem(n2, ROWS), vmem(8, n2, ROWS),
         vmem(n3 + 2, tall), vmem(n3 + 2, tall), vmem(n3 + 2, tall), vmem(n3, ROWS), vmem(8, n3, ROWS),
         vmem(n4 + 2, tall), vmem(n4 + 2, tall), vmem(n4 + 2, tall), vmem(n4, ROWS), vmem(8, n4, ROWS),

time: 38.8 us -> 36.5 us (0.941)
  Pallas kernels: 35.6 us -> 33.3 us
    pallas_call x1, Pallas kernels: 35.6 us -> 33.3 us  [shards(): pl.pallas_call(functools.partial(kernel, sizes), out_shape=(block, block)...]
where the time goes in v3:
time: 36.5 us; the launch traced here: 36.3 us
  Pallas kernels  33.3 us (91%)
  local copies, waits for them, and re-layouts  2.42 us (7%)
  between operations  0.65 us (2%)
    pallas_call x1, Pallas kernels, shards(): pl.pallas_call(functools.partial(kernel, sizes), out_shape=(block, block)...  33.3 us
    unnamed x4, local copies, waits for them, and re-layouts  2.42 us

profile of v3, /device:TPU:1, one launch (start us, length us, event | category | flops | bytes accessed | tf_op | source)
XLA Modules:
  0.0 36.3 jit_solution(1145342801020934749)
XLA Ops:
  0.6 33.3 %vcycle.1 = (f32[16,32,128]{2,1,0:T(8,128)}, f32[16,32,128]{2,1,0:T(8,128)}) custom-call(f32[16,32,128]{2,1,0:T(8,128)} %rhs_hbm.1, f32[16,32,128]{2,1,0:T(8,128)} %permit_hbm.1, f32[16,32,128]{2,1,0:T(8,128)} %guess_hbm.1), custom_call_target="tpu_custom_call" | custom-call | tf_op jit(solution)/shard_map/vcycle/pallas_call | solution.py:933
  33.9 0.0 copy-start
  33.9 1.7 %copy.7 = f32[16,32,128]{2,1,0:T(8,128)} copy(f32[16,32,128]{2,1,0:T(8,128)} %get-tuple-element.4) | data formatting | bytes 524288
  35.6 0.0 copy-done
  35.6 0.7 %copy.8 = f32[16,32,128]{2,1,0:T(8,128)} copy(f32[16,32,128]{2,1,0:T(8,128)S(1)} %copy-done) | data formatting | bytes 524288
Async XLA Ops:
  33.9 1.7 %copy-start = (f32[16,32,128]{2,1,0:T(8,128)S(1)}, f32[16,32,128]{2,1,0:T(8,128)}, u32[]{:S(2)}) copy-start(f32[16,32,128]{2,1,0:T(8,128)} %get-tuple-element.5) | copy-start | bytes 786436

commit v4 on v3

--- a/solution.py
+++ b/solution.py
@@ -127,6 +127,9 @@
 
 SEMS = 104
 
+DOWN_Z, DOWN_TURN = (92, 63, 95, 60), 67
+UP_Z, UP_TURN = (66, 32, 64, 34), 62
+
 
 def pack_z(acc, v, first, w):
     group = iota((8, LANES), 1) // (2 * w)
@@ -175,8 +178,13 @@
 
 
 def pair_sum(v, step, axis):
+    if axis == 0 and v.shape[0] > 8:
+        tiles = [pair_sum(v[i : i + 8], step, 0) for i in range(0, v.shape[0], 8)]
+        return jnp.concatenate(tiles, axis=0)
+    size = v.shape[axis]
+    if 2 * step == size:
+        return v + roll(v, step, axis)
     even = (iota(v.shape, axis) // step) % 2 == 0
-    size = v.shape[axis]
     return v + jnp.where(even, roll(v, size - step, axis), roll(v, step, axis))
 
 
@@ -187,7 +195,7 @@
     rhs, gp, smooth, vn, sol, res, st0, zs0, zr0, part, pack_d, cz,
     xa, ya, za, xd, yd, zd, xf, yf, zf, exy, exz, eyz, pxy, pxz, pyz,
     kx, ky, kz, cxz, cyz, rims, crossed,
-    p1, u1, u1h, v1, rw1, b1, st1, tmp, hw1, rw0, zs1, zr1, pick, spread, lhs, select,
+    p1, u1, u1h, v1, rw1, b1, st1, tmp, hw1, rw0, zs1, zr1, pick, spread, lhs,
     raw_p, raw_b, raw_e, p2, u2, b2, st2, p3, u3, v3, b3, st3, p4, wa, wb, b4, st4, w3, v2, w2,
     local_sems, send_sems, recv_sems,
 ):
@@ -355,16 +363,6 @@
     right = jnp.logical_and(row == 2 * Z2, col < 2)
     spread[:, LANES:] = jnp.logical_or(left, right).astype(F32)
 
-    row, col = iota((LANES, LANES), 0), iota((LANES, LANES), 1)
-    group, place = col // Z2, col % Z2
-    for n, chosen in enumerate((
-        jnp.logical_and(group == 0, row == col + Z2),
-        jnp.logical_and(group == 3, row == col - 3 * Z2),
-        jnp.logical_and(place == 0, row == 3 * Z2 + X2 + group),
-        jnp.logical_and(place == Z2 - 1, row == 3 * Z2 + group),
-    )):
-        select[:, n * LANES : (n + 1) * LANES] = chosen.astype(F32)
-
     def to_compact(parts):
         return lax.dot_general(
             parts, pick[...], (((1,), (0,)), ((), ())),
@@ -381,14 +379,14 @@
     steps = [d for k in range(1, REACH + 1) for d in (k, -k)]
     raw_p[0, :, :, :4] = zeros(nx, 3, 4)
     raw_p[2 * REACH, :, :, 4:] = zeros(nx, 3, 4)
-    raw_e[0, :, :, :12] = zeros(nx, 3, 12)
-    raw_e[2 * REACH, :, :, 12:] = zeros(nx, 3, 12)
+    raw_e[0, :, :, :12] = zeros(nx, 4, 12)
+    raw_e[2 * REACH, :, :, 12:] = zeros(nx, 4, 12)
     for d in steps:
 
         @pl.when(jnp.logical_not(net.there((0, d, 0))))
         def _():
             raw_p[REACH + d] = zeros(nx, 3, 8)
-            raw_e[REACH + d] = zeros(nx, 3, 24)
+            raw_e[REACH + d] = zeros(nx, 4, 24)
 
     for d in signs:
 
@@ -397,13 +395,14 @@
             raw_p[REACH, ix, 1 + d] = zeros(8)
             raw_b[:, 1 + d] = zeros(nx, 24)
 
-    def along_y(raw, first, rows, half):
+    def along_y(raw, first, rows, half, packed=False):
         copies = []
         for d in steps:
             span = pl.ds(first, rows)
             if abs(d) == REACH:
                 span = pl.ds(first + rows - half if d > 0 else first, half)
-            copies.append(net.copy(raw.at[REACH, :, :, span], raw.at[REACH - d, :, :, span], (0, d, 0)))
+            slots = pl.ds(2, 2) if packed and abs(d) > 1 else pl.ds(0, 3)
+            copies.append(net.copy(raw.at[REACH, :, slots, span], raw.at[REACH - d, :, slots, span], (0, d, 0)))
         return copies
 
     raw_p[REACH, ix, 1] = compact(lambda x: p1[x + 1, 8 : 8 + Y1])
@@ -535,10 +534,10 @@
             for k in (2 * x, 2 * x + 1)
         ]
         out = 0.125 * halves(out[0] + out[1], X2 + x)
-        z_out = z_out + jnp.where(lane8 == 3 * Z2 + x, roll(out, 3 * Z2 + x, 1), 0.0)
-        z_out = z_out + jnp.where(lane8 == 3 * Z2 + X2 + x, roll(out, 3 * Z2 + X2 + 1 + x, 1), 0.0)
-    for i, x in ((0, 0), (1, X1 - 1)):
-        lhs[16:, i * LANES : (i + 1) * LANES] = halves(st1[i, x] * u1[x + 1, 8 : 8 + Y1], i)
+        z_out = z_out + jnp.where(lane8 == DOWN_Z[x], roll(out, DOWN_Z[x], 1), 0.0)
+        z_out = z_out + jnp.where(lane8 == UP_Z[x], roll(out, UP_Z[x] + 1, 1), 0.0)
+    for i, x, to in ((0, 0, X2 - 1), (1, X1 - 1, 0)):
+        lhs[16:, to * LANES : (to + 1) * LANES] = halves(st1[i, x] * u1[x + 1, 8 : 8 + Y1], i)
     known = to_compact(lhs[...])
     raw_b[ix, 1, :16] = known[:16]
     raw_b[ix, 1, 16:] = known[16:] + z_out
@@ -612,26 +611,36 @@
     loop(X0, static_y)
 
     wait(b2_xz)
-    crossing = lax.dot_general(
-        raw_b[:, :, 16:].reshape(nx * 24, LANES), select[...], (((1,), (0,)), ((), ())),
-        precision=lax.Precision.HIGHEST, preferred_element_type=F32,
-    ).reshape(nx, 3, 8, 4 * LANES)
-    across = lambda n, xd, zd: crossing[xd, zd, :, n * LANES : (n + 1) * LANES]
+    def one_of(*lanes):
+        return jnp.logical_or(lane8 == lanes[0], lane8 == lanes[1])
+
+    def from_z(xd, zd, turn, straight, turned):
+        f = raw_b[xd, zd, 16:]
+        return jnp.where(straight, f, jnp.where(turned, roll(f, turn, 1), 0.0))
+
+    up_masks = one_of(Z2, 2 * Z2), one_of(0, 3 * Z2)
+    down_masks = one_of(2 * Z2 - 1, 3 * Z2 - 1), one_of(Z2 - 1, 4 * Z2 - 1)
+    near_z = lane8 % Z2 < Z2 // 2
     for xd in range(nx):
+        blocks = []
         for zd in range(3):
             b = raw_b[xd, zd, :8]
             if xd > 0:
-                b = b + across(0, xd - 1, zd)
+                b = b + jnp.where(lane8 < Z2, raw_b[xd - 1, zd, 16:], 0.0)
             if xd < nx - 1:
-                b = b + across(1, xd + 1, zd)
+                b = b + jnp.where(lane8 >= 3 * Z2, raw_b[xd + 1, zd, 16:], 0.0)
             if zd > 0:
-                b = b + across(2, xd, zd - 1)
+                b = b + from_z(xd, zd - 1, UP_TURN, *up_masks)
             if zd < 2:
-                b = b + across(3, xd, zd + 1)
-            raw_e[REACH, xd, zd, 8:16] = b
-            raw_e[REACH, xd, zd, 7:8] = raw_b[xd, zd, 8:9]
-            raw_e[REACH, xd, zd, 16:17] = raw_b[xd, zd, 9:10]
-    b2_y = along_y(raw_e, 7, 10, 5)
+                b = b + from_z(xd, zd + 1, DOWN_TURN, *down_masks)
+            blocks.append((b, raw_b[xd, zd, 8:9], raw_b[xd, zd, 9:10]))
+        low, own, high = blocks
+        both = tuple(jnp.where(near_z[: h.shape[0]], h, l) for l, h in zip(low, high))
+        for n, (b, down_y, up_y) in enumerate((low, high, own, both)):
+            raw_e[REACH, xd, n, 8:16] = b
+            raw_e[REACH, xd, n, 7:8] = down_y
+            raw_e[REACH, xd, n, 16:17] = up_y
+    b2_y = along_y(raw_e, 7, 10, 5, True)
     start(b2_y)
 
     for f in (p2, u2, p3, u3, v3, p4, wa, wb):
@@ -705,13 +714,21 @@
     def unpack_b(xd, _):
         blocks = []
         for zd in range(3):
+
+            def part(yd, rows):
+                if zd == 1 or abs(yd - REACH) < 2:
+                    return raw_e[yd, xd, (0, 2, 1)[zd], rows]
+                v = raw_e[yd, xd, 3, rows]
+                near = near_z[: v.shape[0]]
+                return jnp.where(near, v, 0.0) if zd else jnp.where(near, 0.0, v)
+
             tiles = []
             for yd in range(2 * REACH + 1):
-                b = raw_e[yd, xd, zd, 8:16]
+                b = part(yd, slice(8, 16))
                 if yd > 0:
-                    b = b + jnp.where(row8 == 0, raw_e[yd - 1, xd, zd, 16:17], 0.0)
+                    b = b + jnp.where(row8 == 0, part(yd - 1, slice(16, 17)), 0.0)
                 if yd < 2 * REACH:
-                    b = b + jnp.where(row8 == 7, raw_e[yd + 1, xd, zd, 7:8], 0.0)
+                    b = b + jnp.where(row8 == 7, part(yd + 1, slice(7, 8)), 0.0)
                 tiles.append(b)
             blocks.append(jnp.concatenate(tiles, axis=0))
         for x in range(X2):
@@ -914,8 +931,8 @@
         vmem(*padded1), vmem(*padded1), vmem(*padded1), vmem(*padded1), vmem(*padded1), vmem(X1, Y1), vmem(8, X1, Y1),
         vmem(X1, Y0), vmem(X2, Y1), vmem(X1, Y0), vmem(2, 8), vmem(2, 2, 8),
         vmem(X2 * LANES), pltpu.VMEM((LANES, 2 * LANES), F32),
-        pltpu.VMEM((24, X2 * LANES), F32), pltpu.VMEM((LANES, 4 * LANES), F32),
-        vmem(reach, nx, 3, 8), vmem(nx, 3, 24), vmem(reach, nx, 3, 24),
+        pltpu.VMEM((24, X2 * LANES), F32),
+        vmem(reach, nx, 3, 8), vmem(nx, 3, 24), vmem(reach, nx, 4, 24),
         vmem(n2 + 2, tall), vmem(n2 + 2, tall), vmem(n2, ROWS), vmem(8, n2, ROWS),
         vmem(n3 + 2, tall), vmem(n3 + 2, tall), vmem(n3 + 2, tall), vmem(n3, ROWS), vmem(8, n3, ROWS),
         vmem(n4 + 2, tall), vmem(n4 + 2, tall), vmem(n4 + 2, tall), vmem(n4, ROWS), vmem(8, n4, ROWS),
@@ -937,7 +954,7 @@
             out_specs=[pl.BlockSpec(memory_space=pl.ANY)] * 2,
             scratch_shapes=scratch(sizes[0]),
             compiler_params=pltpu.CompilerParams(
-                collective_id=0, has_side_effects=True, vmem_limit_bytes=60 * 2**20
+                collective_id=0, has_side_effects=True, vmem_limit_bytes=213 * 2**18
             ),
             name="vcycle",
         )(right_side, dielectric, guess)

time: 36.5 us -> 34.2 us (0.937)
  Pallas kernels: 33.3 us -> 32.1 us
  local copies, waits for them, and re-layouts: 2.42 us -> 1.41 us
    pallas_call x1, Pallas kernels: 33.3 us -> 32.1 us  [shards(): pl.pallas_call(functools.partial(kernel, sizes), out_shape=(block, block)...]
    unnamed x4 -> x2, local copies, waits for them, and re-layouts: 2.42 us -> 1.41 us
where the time goes in v4:
time: 34.2 us; the launch traced here: 34.1 us
  Pallas kernels  32.1 us (94%)
  local copies, waits for them, and re-layouts  1.41 us (4%)
  between operations  0.64 us (2%)
    pallas_call x1, Pallas kernels, shards(): pl.pallas_call(functools.partial(kernel, sizes), out_shape=(block, block)...  32.1 us
    unnamed x2, local copies, waits for them, and re-layouts  1.41 us

profile of v4, /device:TPU:1, one launch (start us, length us, event | category | flops | bytes accessed | tf_op | source)
XLA Modules:
  0.0 34.1 jit_solution(17280747994828487377)
XLA Ops:
  0.6 32.1 %vcycle.1 = (f32[16,32,128]{2,1,0:T(8,128)S(1)}, f32[16,32,128]{2,1,0:T(8,128)S(1)}) custom-call(f32[16,32,128]{2,1,0:T(8,128)} %rhs_hbm.1, f32[16,32,128]{2,1,0:T(8,128)} %permit_hbm.1, f32[16,32,128]{2,1,0:T(8,128)} %guess_hbm.1), custom_call_target="tpu_custom_call" | custom-call | tf_op jit(solution)/shard_map/vcycle/pallas_call | solution.py:950
  32.7 0.7 %copy.7 = f32[16,32,128]{2,1,0:T(8,128)} copy(f32[16,32,128]{2,1,0:T(8,128)S(1)} %get-tuple-element.4) | data formatting | bytes 524288
  33.4 0.7 %copy.8 = f32[16,32,128]{2,1,0:T(8,128)} copy(f32[16,32,128]{2,1,0:T(8,128)S(1)} %get-tuple-element.5) | data formatting | bytes 524288

commit v5 on v4

--- a/solution.py
+++ b/solution.py
@@ -55,12 +55,11 @@
             self.copies[(0, 0, d)] = net.copy(sent, got.at[0 if d > 0 else 1], (0, 0, d))
 
     def start(self):
-        for way in ((0, 0, 1), (0, 0, -1), (1, 0, 0), (-1, 0, 0), (0, 1, 0), (0, -1, 0)):
-            self.net.start(self.copies[way])
+        order = ((0, 0, 1), (0, 0, -1), (1, 0, 0), (-1, 0, 0), (0, 1, 0), (0, -1, 0))
+        self.net.start([self.copies[way] for way in order])
 
     def wait(self):
-        for copy in self.copies.values():
-            self.net.wait_recv(copy)
+        self.net.wait_recv(list(self.copies.values()))
 
 
 class Net:
@@ -102,27 +101,37 @@
         )
         return (made, way)
 
-    def start(self, copy):
-        made, way = copy
-        self.started.append(copy)
-
-        @self.when(way)
+    def each(self, copies, act):
+        ways = {way for _, way in copies if any(way)}
+        if not ways:
+            for made, _ in copies:
+                act(made)
+            return
+        found = functools.reduce(jnp.logical_and, [self.there(way) for way in sorted(ways)])
+
+        @pl.when(found)
         def _():
-            made.start()
-
-    def wait_recv(self, copy):
-        made, way = copy
-
-        @self.when(tuple(-d for d in way))
+            for made, _ in copies:
+                act(made)
+
+        @pl.when(jnp.logical_not(found))
         def _():
-            made.wait_recv()
+            for made, way in copies:
+
+                @self.when(way)
+                def _():
+                    act(made)
+
+    def start(self, copies):
+        self.started += copies
+        self.each(copies, lambda made: made.start())
+
+    def wait_recv(self, copies):
+        self.each([(made, tuple(-d for d in way)) for made, way in copies], lambda made: made.wait_recv())
 
     def finish(self):
-        for made, way in self.started:
-
-            @self.when(way)
-            def _():
-                made.wait_send()
+        started, self.started = self.started, []
+        self.each(started, lambda made: made.wait_send())
 
 
 SEMS = 104
@@ -191,8 +200,8 @@
 def kernel(
     sizes,
     rhs_hbm, permit_hbm, guess_hbm,
-    sol_hbm, res_hbm,
-    rhs, gp, smooth, vn, sol, res, st0, zs0, zr0, part, pack_d, cz,
+    sol_ref, res_ref,
+    rhs, gp, smooth, vn, sol, st0, zs0, zr0, part, pack_d, cz,
     xa, ya, za, xd, yd, zd, xf, yf, zf, exy, exz, eyz, pxy, pxz, pyz,
     kx, ky, kz, cxz, cyz, rims, crossed,
     p1, u1, u1h, v1, rw1, b1, st1, tmp, hw1, rw0, zs1, zr1, pick, spread, lhs,
@@ -205,22 +214,22 @@
     inner0 = (pl.ds(1, X0), pl.ds(8, Y0))
     own0 = slice(8, 8 + Y0)
 
+    ways = [(0, 0, 1), (0, 0, -1), (1, 0, 0), (-1, 0, 0), (0, 1, 0), (0, -1, 0)]
+    greeted = ways + [(2, 0, 0), (-2, 0, 0)]
+    barrier = pltpu.get_barrier_semaphore()
+    for way in greeted:
+
+        @net.when(way)
+        def _():
+            pl.semaphore_signal(barrier, inc=1, device_id=net.device(way), device_id_type=MESH)
+
     loads = [
+        pltpu.make_async_copy(permit_hbm, gp.at[(1,) + inner0], local_sems.at[1]),
         pltpu.make_async_copy(guess_hbm, gp.at[(0,) + inner0], local_sems.at[0]),
-        pltpu.make_async_copy(permit_hbm, gp.at[(1,) + inner0], local_sems.at[1]),
         pltpu.make_async_copy(rhs_hbm, rhs, local_sems.at[2]),
     ]
     for load in loads:
         load.start()
-
-    ways = [(0, 0, 1), (0, 0, -1), (1, 0, 0), (-1, 0, 0), (0, 1, 0), (0, -1, 0)]
-    greeted = ways + [(2, 0, 0), (-2, 0, 0)]
-    barrier = pltpu.get_barrier_semaphore()
-    for way in greeted:
-
-        @net.when(way)
-        def _():
-            pl.semaphore_signal(barrier, inc=1, device_id=net.device(way), device_id_type=MESH)
 
     signs = (-1, 1)
     zeros = lambda *shape: jnp.zeros(shape + (LANES,), F32)
@@ -264,10 +273,44 @@
 
     zero_halo(gp, (0,))
     zero_halo(gp, (1,))
+    zero_halo(vn, (0,))
+    zero_halo(u1, (), X1, Y1)
+    lhs[...] = jnp.zeros(lhs.shape, F32)
     clear([], landings(xa, ya, za))
-
-    for load in loads:
-        load.wait()
+    clear([(p1, X1, Y1), (u1h, X1, Y1), (smooth, X0, Y0)], [
+        (zr, (r, i), (0, 0, d)) for zr, n in ((zr1, 2), (zr0, 1)) for r in range(n) for i, d in enumerate(signs)
+    ])
+    for x in range(X2):
+        row, col = iota((LANES, LANES), 0), iota((LANES, LANES), 1)
+        take = jnp.logical_and(col == Z2 * x + row // 4, row % 2 == 0)
+        pick[pl.ds(x * LANES, LANES)] = jnp.where(take, 0.125, 0.0).astype(F32)
+    row, col = iota((LANES, LANES), 0), iota((LANES, LANES), 1)
+    spread[:, :LANES] = (row == Z2 + col // 4).astype(F32).astype(jnp.bfloat16)
+    left = jnp.logical_and(row == Z2 - 1, col >= LANES - 2)
+    right = jnp.logical_and(row == 2 * Z2, col < 2)
+    spread[:, LANES:] = jnp.logical_or(left, right).astype(F32).astype(jnp.bfloat16)
+
+    steps = [d for k in range(REACH, 0, -1) for d in (k, -k)]
+    raw_p[0, :, :, :4] = zeros(nx, 3, 4)
+    raw_p[2 * REACH, :, :, 4:] = zeros(nx, 3, 4)
+    raw_e[0, :, :, :12] = zeros(nx, 4, 12)
+    raw_e[2 * REACH, :, :, 12:] = zeros(nx, 4, 12)
+    for d in steps:
+
+        @pl.when(jnp.logical_not(net.there((0, d, 0))))
+        def _():
+            raw_p[REACH + d] = zeros(nx, 3, 8)
+            raw_e[REACH + d] = zeros(nx, 4, 24)
+
+    for d in signs:
+
+        @pl.when(jnp.logical_not(net.there((0, 0, d))))
+        def _():
+            raw_p[REACH, ix, 1 + d] = zeros(8)
+            raw_b[:, 1 + d] = zeros(nx, 24)
+
+    loads[0].wait()
+    loads[1].wait()
 
     lane0 = iota((Y0, LANES), 1)
 
@@ -282,21 +325,10 @@
     def sum0(x, vs):
         return weighted([st0[i, x] for i in range(6)], vs)
 
-    def first(x, accs):
-        p, ns = inside0(gp, x, (1,))
-        ns = ns[:4] + (jnp.where(lane0 == 0, 0.0, ns[4]), jnp.where(lane0 == LANES - 1, 0.0, ns[5]))
-        cs, diag = couplings(0.5, p, ns)
-        cs[4] = jnp.where(lane0 == 0, 0.0, cs[4])
-        cs[5] = jnp.where(lane0 == LANES - 1, 0.0, cs[5])
-        for i, c in enumerate(cs):
-            st0[i, x] = c
-        st0[6, x] = diag
-        v, vs = inside0(gp, x, (0,))
-        part[x] = rhs[x] + weighted(cs, vs)
-        return pack_z(accs[0], v, 4 * x, 1), pack_z(accs[1], p, 4 * x, 1)
-
     zero = zeros(8)
-    accs = loop(X0, first, (zero, zero))
+    accs = loop(X0, lambda x, accs: tuple(
+        pack_z(a, gp[i, x + 1, 8 : 8 + Y0], 4 * x, 1) for i, a in enumerate(accs)
+    ), (zero, zero))
     zs0[0, 0] = accs[0]
     zs0[0, 1] = accs[1]
 
@@ -325,19 +357,29 @@
                 copies.append(net.copy(line, xy.at[1 - i, 1 - j, pl.ds(0, 1)], (d, e, 0)))
         return copies
 
-    def start(copies):
-        for copy in copies:
-            net.start(copy)
-
-    def wait(copies):
-        for copy in copies:
-            net.wait_recv(copy)
+    start, wait = net.start, net.wait_recv
 
     round_a = face_copies(
         gp, (slice(None),), lambda i: xa.at[i], lambda i: ya.at[i, :, :, pl.ds(0, 1)],
         zs0.at[0], lambda i: za.at[i],
     )
     start(round_a)
+    loads[2].wait()
+
+    def first(x, _):
+        p, ns = inside0(gp, x, (1,))
+        ns = ns[:4] + (jnp.where(lane0 == 0, 0.0, ns[4]), jnp.where(lane0 == LANES - 1, 0.0, ns[5]))
+        cs, diag = couplings(0.5, p, ns)
+        cs[4] = jnp.where(lane0 == 0, 0.0, cs[4])
+        cs[5] = jnp.where(lane0 == LANES - 1, 0.0, cs[5])
+        for i, c in enumerate(cs):
+            st0[i, x] = c
+        st0[6, x] = diag
+        v, vs = inside0(gp, x, (0,))
+        part[x] = rhs[x] + weighted(cs, vs)
+        return 0
+
+    loop(X0, first)
 
     def coarse_p1(x, acc):
         tmp[x] = gp[1, 2 * x + 1, 8 : 8 + Y0] + gp[1, 2 * x + 2, 8 : 8 + Y0]
@@ -346,22 +388,21 @@
         p1[x + 1, 8 : 8 + Y1] = v
         return pack_z(acc, v, 2 * x, 2)
 
-    clear([(p1, X1, Y1), (u1h, X1, Y1), (smooth, X0, Y0)], [
-        (zr, (r, i), (0, 0, d)) for zr, n in ((zr1, 2), (zr0, 1)) for r in range(n) for i, d in enumerate(signs)
-    ])
     zs1[0] = loop(X1, coarse_p1, zero)
     faces_p1 = Faces(net, p1, p1, zs1.at[0], zr1.at[0], X1, Y1)
     faces_p1.start()
 
-    for x in range(X2):
-        row, col = iota((LANES, LANES), 0), iota((LANES, LANES), 1)
-        take = jnp.logical_and(col == Z2 * x + row // 4, row % 2 == 0)
-        pick[pl.ds(x * LANES, LANES)] = jnp.where(take, 0.125, 0.0).astype(F32)
-    row, col = iota((LANES, LANES), 0), iota((LANES, LANES), 1)
-    spread[:, :LANES] = (row == Z2 + col // 4).astype(F32)
-    left = jnp.logical_and(row == Z2 - 1, col >= LANES - 2)
-    right = jnp.logical_and(row == 2 * Z2, col < 2)
-    spread[:, LANES:] = jnp.logical_or(left, right).astype(F32)
+    def exact_dot(v, ref):
+        rows = v.shape[0]
+        high = v.astype(jnp.bfloat16)
+        rest = v - high.astype(F32)
+        middle = rest.astype(jnp.bfloat16)
+        low = (rest - middle.astype(F32)).astype(jnp.bfloat16)
+        out = lax.dot_general(
+            jnp.concatenate([high, middle, low], axis=0), ref[...], (((1,), (0,)), ((), ())),
+            preferred_element_type=F32,
+        )
+        return out[:rows] + (out[rows : 2 * rows] + out[2 * rows :])
 
     def to_compact(parts):
         return lax.dot_general(
@@ -375,25 +416,6 @@
             tmp[x, :Y1] = planes(2 * x) + planes(2 * x + 1)
             parts.append(tmp[x, pl.ds(0, Y2, stride=2)] + tmp[x, pl.ds(1, Y2, stride=2)])
         return to_compact(jnp.concatenate(parts, axis=1))
-
-    steps = [d for k in range(1, REACH + 1) for d in (k, -k)]
-    raw_p[0, :, :, :4] = zeros(nx, 3, 4)
-    raw_p[2 * REACH, :, :, 4:] = zeros(nx, 3, 4)
-    raw_e[0, :, :, :12] = zeros(nx, 4, 12)
-    raw_e[2 * REACH, :, :, 12:] = zeros(nx, 4, 12)
-    for d in steps:
-
-        @pl.when(jnp.logical_not(net.there((0, d, 0))))
-        def _():
-            raw_p[REACH + d] = zeros(nx, 3, 8)
-            raw_e[REACH + d] = zeros(nx, 4, 24)
-
-    for d in signs:
-
-        @pl.when(jnp.logical_not(net.there((0, 0, d))))
-        def _():
-            raw_p[REACH, ix, 1 + d] = zeros(8)
-            raw_b[:, 1 + d] = zeros(nx, 24)
 
     def along_y(raw, first, rows, half, packed=False):
         copies = []
@@ -407,12 +429,7 @@
 
     raw_p[REACH, ix, 1] = compact(lambda x: p1[x + 1, 8 : 8 + Y1])
     p2_z = [net.copy(raw_p.at[REACH, ix, 1], raw_p.at[REACH, ix, 1 - d], (0, 0, d)) for d in (1, -1)]
-    for copy in p2_z:
-        net.start(copy)
-    zero_halo(vn, (0,))
-    zero_halo(u1, (), X1, Y1)
-    lhs[...] = jnp.zeros(lhs.shape, F32)
-
+    start(p2_z)
     wait(round_a)
     own_p = zs0[0, 1]
     cross_p = cross_z(za[0, 1], za[1, 1])
@@ -474,8 +491,7 @@
 
     pack_d[...] = loop(X0, lambda x, acc: pack_z(acc, st0[6, x], 4 * x, 1), zero)
 
-    for copy in p2_z:
-        net.wait_recv(copy)
+    wait(p2_z)
     p2_x = [net.copy(raw_p.at[REACH, ix], raw_p.at[REACH, ix], (0, 0, 0), k) for k in range(1, nx)]
     start(p2_x)
 
@@ -497,8 +513,11 @@
 
     sum_s = cz[...] * cross_z(zr0[0, 0], zr0[0, 1])
 
+    def remainders0(x, _):
+        tmp[x] = remainder0(smooth, 2 * x, sum_s) + remainder0(smooth, 2 * x + 1, sum_s)
+        return 0
+
     def down0(x, acc):
-        tmp[x] = remainder0(smooth, 2 * x, sum_s) + remainder0(smooth, 2 * x + 1, sum_s)
         b = tmp[x, pl.ds(0, Y1, stride=2)] + tmp[x, pl.ds(1, Y1, stride=2)]
         b = 0.125 * pair_sum(b, 1, 1)
         b1[x] = b
@@ -506,6 +525,7 @@
         u1[x + 1, 8 : 8 + Y1] = u
         return pack_z(acc, u, 2 * x, 2)
 
+    loop(X1, remainders0)
     zs1[1] = loop(X1, down0, zero)
 
 
@@ -516,28 +536,35 @@
         u, us = sides1(u1, x, nothing)
         return b1[x] - st1[6, x] * u + weighted([st1[i, x] for i in range(6)], us)
 
-    def halves(v, at):
-        tmp[at, :Y1] = v
+    def halve(at):
         return tmp[at, pl.ds(0, Y2, stride=2)] + tmp[at, pl.ds(1, Y2, stride=2)]
 
     lane8 = iota((8, LANES), 1)
     z_out = zero
     for x in range(X2):
-        cols = pl.ds(x * LANES, LANES)
-        lhs[:8, cols] = halves(remainder1(2 * x) + remainder1(2 * x + 1), x)
-        for i, y in ((0, 0), (1, Y1 - 1)):
-            lhs[8 + i : 9 + i, cols] = sum(
-                st1[2 + i, k, y : y + 1] * u1[k + 1, 8 + y : 9 + y] for k in (2 * x, 2 * x + 1)
-            )
+        pair = (2 * x, 2 * x + 1)
+        tmp[x, :Y1] = remainder1(pair[0]) + remainder1(pair[1])
         out = [
             jnp.where(lane16 == 0, st1[4, k], jnp.where(lane16 == LANES - 1, st1[5, k], 0.0)) * u1[k + 1, 8 : 8 + Y1]
-            for k in (2 * x, 2 * x + 1)
+            for k in pair
         ]
-        out = 0.125 * halves(out[0] + out[1], X2 + x)
+        tmp[X2 + x, :Y1] = out[0] + out[1]
+        for i, y in ((0, 0), (1, Y1 - 1)):
+            lhs[8 + i : 9 + i, x * LANES : (x + 1) * LANES] = sum(
+                st1[2 + i, k, y : y + 1] * u1[k + 1, 8 + y : 9 + y] for k in pair
+            )
+    x_out = ((0, 0, X2 - 1), (1, X1 - 1, 0))
+    for i, x, _ in x_out:
+        tmp[i, Y1:] = st1[i, x] * u1[x + 1, 8 : 8 + Y1]
+    for x in range(X2):
+        lhs[:8, x * LANES : (x + 1) * LANES] = halve(x)
+        out = 0.125 * halve(X2 + x)
         z_out = z_out + jnp.where(lane8 == DOWN_Z[x], roll(out, DOWN_Z[x], 1), 0.0)
         z_out = z_out + jnp.where(lane8 == UP_Z[x], roll(out, UP_Z[x] + 1, 1), 0.0)
-    for i, x, to in ((0, 0, X2 - 1), (1, X1 - 1, 0)):
-        lhs[16:, to * LANES : (to + 1) * LANES] = halves(st1[i, x] * u1[x + 1, 8 : 8 + Y1], i)
+    for i, _, to in x_out:
+        lhs[16:, to * LANES : (to + 1) * LANES] = (
+            tmp[i, pl.ds(Y1, Y2, stride=2)] + tmp[i, pl.ds(Y1 + 1, Y2, stride=2)]
+        )
     known = to_compact(lhs[...])
     raw_b[ix, 1, :16] = known[:16]
     raw_b[ix, 1, 16:] = known[16:] + z_out
@@ -545,7 +572,7 @@
     mine = raw_b.at[ix, 1]
     b2_xz = []
     for d in (1, -1, 0):
-        for k in range(nx):
+        for k in sorted(range(nx), key=lambda k: -min(k, nx - k)):
             if d or k:
                 b2_xz.append(net.copy(mine, raw_b.at[ix, 1 - d], (0, 0, d), k))
     start(b2_xz)
@@ -553,8 +580,7 @@
     round_c = Faces(net, u1, u1h, zs1.at[1], zr1.at[1], X1, Y1)
     round_c.start()
 
-    for copy in p2_x:
-        net.wait_recv(copy)
+    wait(p2_x)
     p2_y = along_y(raw_p, 0, 8, 4)
     start(p2_y)
 
@@ -662,8 +688,7 @@
         part = [roll(blocks[zd], Z2 * (zd - x), 1) for zd in range(3)]
         return jnp.where(lane < Z2, part[0], jnp.where(lane < 2 * Z2, part[1], jnp.where(lane < 3 * Z2, part[2], 0.0)))
 
-    for copy in p2_y:
-        net.wait_recv(copy)
+    wait(p2_y)
 
     def unpack_p(xd, _):
         blocks = [raw_p[:, xd, zd].reshape(ROWS, LANES) for zd in range(3)]
@@ -708,8 +733,8 @@
     couple_region(p3, st3, 2, 0.5 / 64)
     couple_region(p4, st4, 4, 0.5 / 256)
 
-    for copy in b2_y:
-        net.wait_recv(copy)
+    net.finish()
+    wait(b2_y)
 
     def unpack_b(xd, _):
         blocks = []
@@ -745,13 +770,17 @@
         return b_ref[x] - st[6, x] * u + weighted([st[i, x] for i in range(6)], us)
 
     def down(u_ref, b_ref, st, step, next_b, next_u, next_st):
+        def sums(x, _):
+            next_b[x] = remainder(u_ref, b_ref, st, 2 * x, step) + remainder(u_ref, b_ref, st, 2 * x + 1, step)
+            return 0
+
         def one(x, _):
-            r = remainder(u_ref, b_ref, st, 2 * x, step) + remainder(u_ref, b_ref, st, 2 * x + 1, step)
-            b = coarse(r, step)
+            b = coarse(next_b[x], step)
             next_b[x] = b
             next_u[x + 1, 8 : 8 + ROWS] = next_st[7, x] * b
             return 0
 
+        loop(next_b.shape[0], sums)
         loop(next_b.shape[0], one)
 
     down(u2, b2, st2, 1, b3, u3, st3)
@@ -796,10 +825,8 @@
 
     loop(4 * nx, relax2)
 
-    wide = lax.dot_general(
-        w2[pl.ds(X2 * ix, X2 + 2)].reshape((X2 + 2) * span, LANES), spread[...], (((1,), (0,)), ((), ())),
-        precision=lax.Precision.HIGHEST, preferred_element_type=F32,
-    ).reshape(X2 + 2, span, 2 * LANES)
+    wide = exact_dot(w2[pl.ds(X2 * ix, X2 + 2)].reshape((X2 + 2) * span, LANES), spread)
+    wide = wide.reshape(X2 + 2, span, 2 * LANES)
     for x in range(X1 + 2):
         m = wide[(x + 1) // 2, :, :LANES]
         rw1[x, pl.ds(8, Y2, stride=2)] = m[8 : 8 + Y2]
@@ -820,42 +847,46 @@
         hw1[x, pl.ds(0, Y2, stride=2)] = h
         hw1[x, pl.ds(1, Y2, stride=2)] = h
 
-    def up1(x, acc):
+    def up1(x, _):
         halo = unpack_z(both_u, 2 * x, 2, 2) + hw1[x // 2]
         v, vs = sides1(v1, x, halo)
         w = (1.0 - OMEGA) * v + st1[7, x] * (b1[x] + weighted([st1[i, x] for i in range(6)], vs))
         rw0[x, pl.ds(0, Y1, stride=2)] = w
         rw0[x, pl.ds(1, Y1, stride=2)] = w
+        return 0
+
+    def v_from(x, acc):
         for d in range(2):
             v = smooth[2 * x + d + 1, own0] + rw0[x]
             vn[0, 2 * x + d + 1, own0] = v
             acc = pack_z(acc, v, 4 * (2 * x + d), 1)
         return acc
 
-    zs0[2, 0] = loop(X1, up1, zero)
-
+    loop(X1, up1)
+    zs0[2, 0] = loop(X1, v_from, zero)
+
+    z_ways = ((1, 1), (0, -1))
     round_f = edge_copies(vn, (0,), zs0.at[2, 0], exy, exz, eyz)
-    round_f += face_copies(
-        vn, (0,), lambda i: xf.at[i, 0], lambda i: yf.at[i, 0, :, pl.ds(0, 1)],
-        zs0.at[2, 0], lambda i: zf.at[i, 0],
-    )
+    round_f[8:8] = [net.copy(zs0.at[2, 0], zf.at[1 - i, 0], (0, 0, d)) for i, d in z_ways]
     start(round_f)
 
     def last_part(x, acc):
         _, vs = inside0(vn, x, (0,))
         n = rhs[x] + sum0(x, vs)
-        vn[1, x + 1, own0] = n
         part[x] = n
         return pack_z(acc, n, 4 * x, 1)
 
     zs0[2, 1] = loop(X0, last_part, zero)
+    for x in (0, X0 - 1):
+        vn[1, x + 1, own0] = part[x]
+    for y in (0, Y0 - 1):
+        vn[1, 1 : X0 + 1, 8 + y : 9 + y] = part[:, y : y + 1]
     round_n = face_copies(
-        vn, (1,), lambda i: xf.at[i, 1], lambda i: yf.at[i, 1, :, pl.ds(0, 1)],
+        vn, (slice(None),), lambda i: xf.at[i], lambda i: yf.at[i, :, :, pl.ds(0, 1)],
         zs0.at[2, 1], lambda i: zf.at[i, 1],
     )
     start(round_n)
-    wait(round_f)
-    wait(round_n)
+    wait(round_f + round_n)
 
     edge_x = [cross_z(exz[i, 0], exz[i, 1]) for i in range(2)]
     edge_y = [cross_z(eyz[i, 0], eyz[i, 1]) for i in range(2)]
@@ -894,23 +925,19 @@
 
     def last_z(x, _):
         n = part[x] + at_edges(z_part, 4 * x, 4)
-        sol[x + 1, own0] = (1.0 - OMEGA) * vn[0, x + 1, own0] + st0[7, x] * n
+        s = (1.0 - OMEGA) * vn[0, x + 1, own0] + st0[7, x] * n
+        sol[x + 1, own0] = s
+        sol_ref[x] = s
         return 0
 
     loop(X0, last_z)
-    out_sol = pltpu.make_async_copy(sol.at[inner0], sol_hbm, local_sems.at[3])
-    out_sol.start()
 
     def residual(x, _):
-        res[x] = remainder0(sol, x, sum_x)
+        res_ref[x] = remainder0(sol, x, sum_x)
         return 0
 
     loop(X0, residual)
-    out_res = pltpu.make_async_copy(res, res_hbm, local_sems.at[4])
-    out_res.start()
     net.finish()
-    out_sol.wait()
-    out_res.wait()
 
 
 def scratch(nx):
@@ -922,7 +949,7 @@
     n2, n3, n4, tall = 4 * nx, 2 * nx, nx, ROWS + 16
     reach = 2 * REACH + 1
     return [
-        vmem(X0, Y0), vmem(2, *padded0), vmem(*padded0), vmem(2, *padded0), vmem(*padded0), vmem(X0, Y0),
+        vmem(X0, Y0), vmem(2, *padded0), vmem(*padded0), vmem(2, *padded0), vmem(*padded0),
         vmem(8, X0, Y0), vmem(3, 2, 8), vmem(1, 2, 8), vmem(X0, Y0), vmem(8), vmem(8),
         vmem(2, 2, Y0), vmem(2, 2, X0, 8), vmem(2, 2, 8), vmem(2, Y0), vmem(2, X0, 8), vmem(2, 8),
         vmem(2, 2, Y0), vmem(2, 2, X0, 8), vmem(2, 2, 8),
@@ -930,14 +957,14 @@
         vmem(2, Y0), vmem(2, X0, 8), vmem(8), vmem(2, Y0), vmem(2, X0, 8), vmem(12, 8), vmem(2, 8),
         vmem(*padded1), vmem(*padded1), vmem(*padded1), vmem(*padded1), vmem(*padded1), vmem(X1, Y1), vmem(8, X1, Y1),
         vmem(X1, Y0), vmem(X2, Y1), vmem(X1, Y0), vmem(2, 8), vmem(2, 2, 8),
-        vmem(X2 * LANES), pltpu.VMEM((LANES, 2 * LANES), F32),
+        vmem(X2 * LANES), pltpu.VMEM((LANES, 2 * LANES), jnp.bfloat16),
         pltpu.VMEM((24, X2 * LANES), F32),
         vmem(reach, nx, 3, 8), vmem(nx, 3, 24), vmem(reach, nx, 4, 24),
         vmem(n2 + 2, tall), vmem(n2 + 2, tall), vmem(n2, ROWS), vmem(8, n2, ROWS),
         vmem(n3 + 2, tall), vmem(n3 + 2, tall), vmem(n3 + 2, tall), vmem(n3, ROWS), vmem(8, n3, ROWS),
         vmem(n4 + 2, tall), vmem(n4 + 2, tall), vmem(n4 + 2, tall), vmem(n4, ROWS), vmem(8, n4, ROWS),
         vmem(n3, 24), vmem(n2 + 2, 40), vmem(n2 + 2, 24),
-        pltpu.SemaphoreType.DMA((5,)), pltpu.SemaphoreType.DMA((SEMS,)), pltpu.SemaphoreType.DMA((SEMS,)),
+        pltpu.SemaphoreType.DMA((3,)), pltpu.SemaphoreType.DMA((SEMS,)), pltpu.SemaphoreType.DMA((SEMS,)),
     ]
 
 
@@ -951,7 +978,7 @@
             functools.partial(kernel, sizes),
             out_shape=(block, block),
             in_specs=[pl.BlockSpec(memory_space=pl.ANY)] * 3,
-            out_specs=[pl.BlockSpec(memory_space=pl.ANY)] * 2,
+            out_specs=[pl.BlockSpec(memory_space=pltpu.VMEM)] * 2,
             scratch_shapes=scratch(sizes[0]),
             compiler_params=pltpu.CompilerParams(
                 collective_id=0, has_side_effects=True, vmem_limit_bytes=213 * 2**18

time: 34.2 us -> 33.1 us (0.968)
  Pallas kernels: 32.1 us -> 31 us
    pallas_call x1, Pallas kernels: 32.1 us -> 31 us  [shards(): pl.pallas_call(functools.partial(kernel, sizes), out_shape=(block, block)...]
where the time goes in v5:
time: 33.1 us; the launch traced here: 33 us
  Pallas kernels  31 us (94%)
  local copies, waits for them, and re-layouts  1.41 us (4%)
  between operations  0.64 us (2%)
    pallas_call x1, Pallas kernels, shards(): pl.pallas_call(functools.partial(kernel, sizes), out_shape=(block, block)...  31 us
    unnamed x2, local copies, waits for them, and re-layouts  1.41 us

profile of v5, /device:TPU:1, one launch (start us, length us, event | category | flops | bytes accessed | tf_op | source)
XLA Modules:
  0.0 33.0 jit_solution(4431079234802775076)
XLA Ops:
  0.6 31.0 %vcycle.1 = (f32[16,32,128]{2,1,0:T(8,128)S(1)}, f32[16,32,128]{2,1,0:T(8,128)S(1)}) custom-call(f32[16,32,128]{2,1,0:T(8,128)} %rhs_hbm.1, f32[16,32,128]{2,1,0:T(8,128)} %permit_hbm.1, f32[16,32,128]{2,1,0:T(8,128)} %guess_hbm.1), custom_call_target="tpu_custom_call" | custom-call | tf_op jit(solution)/shard_map/vcycle/pallas_call | solution.py:977
  31.6 0.7 %copy.7 = f32[16,32,128]{2,1,0:T(8,128)} copy(f32[16,32,128]{2,1,0:T(8,128)S(1)} %get-tuple-element.4) | data formatting | bytes 524288
  32.3 0.7 %copy.8 = f32[16,32,128]{2,1,0:T(8,128)} copy(f32[16,32,128]{2,1,0:T(8,128)S(1)} %get-tuple-element.5) | data formatting | bytes 524288

commit v6 on v5

--- a/solution.py
+++ b/solution.py
@@ -285,10 +285,10 @@
         take = jnp.logical_and(col == Z2 * x + row // 4, row % 2 == 0)
         pick[pl.ds(x * LANES, LANES)] = jnp.where(take, 0.125, 0.0).astype(F32)
     row, col = iota((LANES, LANES), 0), iota((LANES, LANES), 1)
-    spread[:, :LANES] = (row == Z2 + col // 4).astype(F32).astype(jnp.bfloat16)
+    spread[:, :LANES] = (row == Z2 + col // 4).astype(F32)
     left = jnp.logical_and(row == Z2 - 1, col >= LANES - 2)
     right = jnp.logical_and(row == 2 * Z2, col < 2)
-    spread[:, LANES:] = jnp.logical_or(left, right).astype(F32).astype(jnp.bfloat16)
+    spread[:, LANES:] = jnp.logical_or(left, right).astype(F32)
 
     steps = [d for k in range(REACH, 0, -1) for d in (k, -k)]
     raw_p[0, :, :, :4] = zeros(nx, 3, 4)
@@ -391,18 +391,6 @@
     zs1[0] = loop(X1, coarse_p1, zero)
     faces_p1 = Faces(net, p1, p1, zs1.at[0], zr1.at[0], X1, Y1)
     faces_p1.start()
-
-    def exact_dot(v, ref):
-        rows = v.shape[0]
-        high = v.astype(jnp.bfloat16)
-        rest = v - high.astype(F32)
-        middle = rest.astype(jnp.bfloat16)
-        low = (rest - middle.astype(F32)).astype(jnp.bfloat16)
-        out = lax.dot_general(
-            jnp.concatenate([high, middle, low], axis=0), ref[...], (((1,), (0,)), ((), ())),
-            preferred_element_type=F32,
-        )
-        return out[:rows] + (out[rows : 2 * rows] + out[2 * rows :])
 
     def to_compact(parts):
         return lax.dot_general(
@@ -825,8 +813,10 @@
 
     loop(4 * nx, relax2)
 
-    wide = exact_dot(w2[pl.ds(X2 * ix, X2 + 2)].reshape((X2 + 2) * span, LANES), spread)
-    wide = wide.reshape(X2 + 2, span, 2 * LANES)
+    wide = lax.dot_general(
+        w2[pl.ds(X2 * ix, X2 + 2)].reshape((X2 + 2) * span, LANES), spread[...], (((1,), (0,)), ((), ())),
+        precision=lax.Precision.HIGHEST, preferred_element_type=F32,
+    ).reshape(X2 + 2, span, 2 * LANES)
     for x in range(X1 + 2):
         m = wide[(x + 1) // 2, :, :LANES]
         rw1[x, pl.ds(8, Y2, stride=2)] = m[8 : 8 + Y2]
@@ -957,7 +947,7 @@
         vmem(2, Y0), vmem(2, X0, 8), vmem(8), vmem(2, Y0), vmem(2, X0, 8), vmem(12, 8), vmem(2, 8),
         vmem(*padded1), vmem(*padded1), vmem(*padded1), vmem(*padded1), vmem(*padded1), vmem(X1, Y1), vmem(8, X1, Y1),
         vmem(X1, Y0), vmem(X2, Y1), vmem(X1, Y0), vmem(2, 8), vmem(2, 2, 8),
-        vmem(X2 * LANES), pltpu.VMEM((LANES, 2 * LANES), jnp.bfloat16),
+        vmem(X2 * LANES), pltpu.VMEM((LANES, 2 * LANES), F32),
         pltpu.VMEM((24, X2 * LANES), F32),
         vmem(reach, nx, 3, 8), vmem(nx, 3, 24), vmem(reach, nx, 4, 24),
         vmem(n2 + 2, tall), vmem(n2 + 2, tall), vmem(n2, ROWS), vmem(8, n2, ROWS),

time: 33.1 us -> 33.2 us (level)
  no operation moved by 1% of the time
where the time goes in v6:
time: 33.2 us; the launch traced here: 33.1 us
  Pallas kernels  31 us (93%)
  local copies, waits for them, and re-layouts  1.41 us (4%)
  between operations  0.64 us (2%)
    pallas_call x1, Pallas kernels, shards(): pl.pallas_call(functools.partial(kernel, sizes), out_shape=(block, block)...  31 us
    unnamed x2, local copies, waits for them, and re-layouts  1.41 us

profile of v6, /device:TPU:1, one launch (start us, length us, event | category | flops | bytes accessed | tf_op | source)
XLA Modules:
  0.0 33.1 jit_solution(2525666085100236005)
XLA Ops:
  0.6 31.0 %vcycle.1 = (f32[16,32,128]{2,1,0:T(8,128)S(1)}, f32[16,32,128]{2,1,0:T(8,128)S(1)}) custom-call(f32[16,32,128]{2,1,0:T(8,128)} %rhs_hbm.1, f32[16,32,128]{2,1,0:T(8,128)} %permit_hbm.1, f32[16,32,128]{2,1,0:T(8,128)} %guess_hbm.1), custom_call_target="tpu_custom_call" | custom-call | tf_op jit(solution)/shard_map/vcycle/pallas_call | solution.py:967
  31.7 0.7 %copy.7 = f32[16,32,128]{2,1,0:T(8,128)} copy(f32[16,32,128]{2,1,0:T(8,128)S(1)} %get-tuple-element.4) | data formatting | bytes 524288
  32.4 0.7 %copy.8 = f32[16,32,128]{2,1,0:T(8,128)} copy(f32[16,32,128]{2,1,0:T(8,128)S(1)} %get-tuple-element.5) | data formatting | bytes 524288

commit v7 on v6

--- a/solution.py
+++ b/solution.py
@@ -293,8 +293,8 @@
     steps = [d for k in range(REACH, 0, -1) for d in (k, -k)]
     raw_p[0, :, :, :4] = zeros(nx, 3, 4)
     raw_p[2 * REACH, :, :, 4:] = zeros(nx, 3, 4)
-    raw_e[0, :, :, :12] = zeros(nx, 4, 12)
-    raw_e[2 * REACH, :, :, 12:] = zeros(nx, 4, 12)
+    raw_e[0, :, :, :13] = zeros(nx, 4, 13)
+    raw_e[2 * REACH, :, :, 11:] = zeros(nx, 4, 13)
     for d in steps:
 
         @pl.when(jnp.logical_not(net.there((0, d, 0))))
@@ -554,15 +554,15 @@
             tmp[i, pl.ds(Y1, Y2, stride=2)] + tmp[i, pl.ds(Y1 + 1, Y2, stride=2)]
         )
     known = to_compact(lhs[...])
-    raw_b[ix, 1, :16] = known[:16]
-    raw_b[ix, 1, 16:] = known[16:] + z_out
-
-    mine = raw_b.at[ix, 1]
+    raw_b[ix, 1, :10] = known[:10]
+    raw_b[ix, 1, 10:18] = known[16:] + z_out
+
+    mine = raw_b.at[ix, 1, pl.ds(0, 18)]
     b2_xz = []
     for d in (1, -1, 0):
         for k in sorted(range(nx), key=lambda k: -min(k, nx - k)):
             if d or k:
-                b2_xz.append(net.copy(mine, raw_b.at[ix, 1 - d], (0, 0, d), k))
+                b2_xz.append(net.copy(mine, raw_b.at[ix, 1 - d, pl.ds(0, 18)], (0, 0, d), k))
     start(b2_xz)
 
     round_c = Faces(net, u1, u1h, zs1.at[1], zr1.at[1], X1, Y1)
@@ -629,7 +629,7 @@
         return jnp.logical_or(lane8 == lanes[0], lane8 == lanes[1])
 
     def from_z(xd, zd, turn, straight, turned):
-        f = raw_b[xd, zd, 16:]
+        f = raw_b[xd, zd, 10:18]
         return jnp.where(straight, f, jnp.where(turned, roll(f, turn, 1), 0.0))
 
     up_masks = one_of(Z2, 2 * Z2), one_of(0, 3 * Z2)
@@ -640,9 +640,9 @@
         for zd in range(3):
             b = raw_b[xd, zd, :8]
             if xd > 0:
-                b = b + jnp.where(lane8 < Z2, raw_b[xd - 1, zd, 16:], 0.0)
+                b = b + jnp.where(lane8 < Z2, raw_b[xd - 1, zd, 10:18], 0.0)
             if xd < nx - 1:
-                b = b + jnp.where(lane8 >= 3 * Z2, raw_b[xd + 1, zd, 16:], 0.0)
+                b = b + jnp.where(lane8 >= 3 * Z2, raw_b[xd + 1, zd, 10:18], 0.0)
             if zd > 0:
                 b = b + from_z(xd, zd - 1, UP_TURN, *up_masks)
             if zd < 2:
@@ -654,7 +654,7 @@
             raw_e[REACH, xd, n, 8:16] = b
             raw_e[REACH, xd, n, 7:8] = down_y
             raw_e[REACH, xd, n, 16:17] = up_y
-    b2_y = along_y(raw_e, 7, 10, 5, True)
+    b2_y = along_y(raw_e, 7, 10, 4, True)
     start(b2_y)
 
     for f in (p2, u2, p3, u3, v3, p4, wa, wb):

time: 33.2 us -> 33.1 us (level)
  no operation moved by 1% of the time
where the time goes in v7:
time: 33.1 us; the launch traced here: 33 us
  Pallas kernels  30.9 us (93%)
  local copies, waits for them, and re-layouts  1.41 us (4%)
  between operations  0.64 us (2%)
    pallas_call x1, Pallas kernels, shards(): pl.pallas_call(functools.partial(kernel, sizes), out_shape=(block, block)...  30.9 us
    unnamed x2, local copies, waits for them, and re-layouts  1.41 us

profile of v7, /device:TPU:1, one launch (start us, length us, event | category | flops | bytes accessed | tf_op | source)
XLA Modules:
  0.0 33.0 jit_solution(18053900185012266086)
XLA Ops:
  0.6 30.9 %vcycle.1 = (f32[16,32,128]{2,1,0:T(8,128)S(1)}, f32[16,32,128]{2,1,0:T(8,128)S(1)}) custom-call(f32[16,32,128]{2,1,0:T(8,128)} %rhs_hbm.1, f32[16,32,128]{2,1,0:T(8,128)} %permit_hbm.1, f32[16,32,128]{2,1,0:T(8,128)} %guess_hbm.1), custom_call_target="tpu_custom_call" | custom-call | tf_op jit(solution)/shard_map/vcycle/pallas_call | solution.py:967
  31.5 0.7 %copy.7 = f32[16,32,128]{2,1,0:T(8,128)} copy(f32[16,32,128]{2,1,0:T(8,128)S(1)} %get-tuple-element.4) | data formatting | bytes 524288
  32.3 0.7 %copy.8 = f32[16,32,128]{2,1,0:T(8,128)} copy(f32[16,32,128]{2,1,0:T(8,128)S(1)} %get-tuple-element.5) | data formatting | bytes 524288
